TPU v7x, 512 devices: a whole 4x4x16 slice. The times are simulated.
512 devices in a mesh: gx: 32 (over z, core), gy: 16 (over x, y).
Axes of the slice: x: 4, y: 4, z: 16, core: 2. Of those that a mesh axis runs over, the one named last changes fastest.
Arguments:
- fields: float32 [4, 4, 4096, 2048], P(None, None, 'gx', 'gy'), may hold values from -6.5 to 6.5
- inv_dx: float32 [4096], P('gx'), may hold values from 0.5 to 2
- inv_dy: float32 [2048], P('gy'), may hold values from 0.5 to 2
Outputs:
- x_derivs: float32 [4, 4, 4096, 2048], P(None, None, 'gx', 'gy')
- y_derivs: float32 [4, 4, 4096, 2048], P(None, None, 'gx', 'gy')
All inputs are finite; a program needn't handle non-finite values.
Results may differ from a plain program's by a relative error of at most 0.00013.
Values sent between devices are 32-bit elements; how exact they have to be, the bound alone decides.
A program may use at most 64 MiB of HBM per device.

v0:
```python
import jax
import jax.numpy as jnp
import numpy as np
from jax import lax
from jax.sharding import PartitionSpec as P

alpha_coef = 4.0 / 9.0
beta_coef = 1.0 / 36.0
near_coef = 20.0 / 27.0
far_coef = 25.0 / 216.0
highest = lax.Precision.HIGHEST


def passed_along(array, axis, by):
    devices = lax.axis_size(axis)
    return lax.ppermute(array, axis, [(i, (i + by) % devices) for i in range(devices)])


def with_halo(cells, sides, width):
    for axis, dim in sides:
        count = lax.axis_size(axis)
        head = lax.slice_in_dim(cells, 0, width, axis=dim)
        tail = lax.slice_in_dim(cells, cells.shape[dim] - width, cells.shape[dim], axis=dim)
        cells = jnp.concatenate(
            [
                lax.ppermute(tail, axis, [(i, (i + 1) % count) for i in range(count)]),
                cells,
                lax.ppermute(head, axis, [((i + 1) % count, i) for i in range(count)]),
            ],
            axis=dim,
        )
    return cells


def invert_table(matrix):
    matrix_order = matrix.shape[0]
    augmented = np.concatenate([np.array(matrix), np.eye(matrix_order)], axis=1)
    for column in range(matrix_order):
        pivot_row = column + int(np.argmax(np.abs(augmented[column:, column])))
        augmented[[column, pivot_row]] = augmented[[pivot_row, column]]
        augmented[column] = augmented[column] / augmented[column, column]
        factor_col = augmented[:, column].copy()
        factor_col[column] = 0.0
        augmented = augmented - np.outer(factor_col, augmented[column])
    return augmented[:, matrix_order:]


def line_tables(cell_count, groups, courant):
    lower_two = beta_coef - courant * far_coef
    lower_one = alpha_coef - courant * near_coef
    upper_one = alpha_coef + courant * near_coef
    upper_two = beta_coef + courant * far_coef
    band = np.eye(cell_count)
    band = band + upper_one * np.eye(cell_count, k=1) + lower_one * np.eye(cell_count, k=-1)
    band = band + upper_two * np.eye(cell_count, k=2) + lower_two * np.eye(cell_count, k=-2)
    inverse = invert_table(band)
    left_edge = np.concatenate(
        [np.array([[lower_two, lower_one], [0.0, lower_two]]), np.zeros((cell_count - 2, 2))],
        axis=0,
    )
    right_edge = np.concatenate(
        [np.zeros((cell_count - 2, 2)), np.array([[upper_two, 0.0], [upper_one, upper_two]])],
        axis=0,
    )
    from_left = inverse @ left_edge
    from_right = inverse @ right_edge
    left_rows = np.concatenate([from_left[:2], from_left[-2:]], axis=0)
    right_rows = np.concatenate([from_right[:2], from_right[-2:]], axis=0)
    lower_block = np.concatenate([np.zeros((4, 2)), left_rows], axis=1)
    upper_block = np.concatenate([right_rows, np.zeros((4, 2))], axis=1)
    levels = []
    coef_low, coef_mid, coef_up = (lower_block, np.eye(4), upper_block)
    distance = 1
    while distance < groups:
        mid_inverse = invert_table(coef_mid)
        left_factor = -coef_low @ mid_inverse
        right_factor = -coef_up @ mid_inverse
        levels.append(
            (
                distance,
                jnp.asarray(left_factor, dtype=jnp.float32),
                jnp.asarray(right_factor, dtype=jnp.float32),
            )
        )
        coef_low, coef_mid, coef_up = (
            left_factor @ coef_low,
            coef_mid + left_factor @ coef_up + right_factor @ coef_low,
            right_factor @ coef_up,
        )
        distance = distance * 2
    closing = invert_table(coef_low + coef_mid + coef_up)
    shift_prev = np.roll(np.eye(groups), -1, axis=1)
    shift_next = np.roll(np.eye(groups), 1, axis=1)
    reduced = (
        np.eye(4 * groups) + np.kron(shift_prev, lower_block) + np.kron(shift_next, upper_block)
    )
    solved_four = invert_table(reduced).reshape(groups, 4, groups, 4)
    weights = np.concatenate(
        [solved_four[groups - 1, 2:4], solved_four[1 % groups, 0:2]], axis=0
    ).transpose(1, 0, 2)
    return (
        jnp.asarray(inverse, dtype=jnp.float32),
        jnp.asarray(from_left, dtype=jnp.float32),
        jnp.asarray(from_right, dtype=jnp.float32),
        levels,
        jnp.asarray(closing, dtype=jnp.float32),
        jnp.asarray(weights, dtype=jnp.float32),
    )


def apply_small(matrix, values):
    return jnp.einsum("ab,bl->al", matrix, values, precision=highest)


def reduce_chain(values, levels, closing, lower_fn, upper_fn):
    for distance, left_factor, right_factor in levels:
        from_below = lower_fn(values, distance)
        from_above = upper_fn(values, distance)
        values = (
            values + apply_small(left_factor, from_below) + apply_small(right_factor, from_above)
        )
    solved = apply_small(closing, values)
    prev_tail = lower_fn(solved[2:4], 1)
    next_head = upper_fn(solved[0:2], 1)
    return (prev_tail, next_head)


def lower_gx(values, distance):
    return passed_along(values, "gx", distance)


def upper_gx(values, distance):
    return passed_along(values, "gx", -distance)


def lower_gy(values, distance):
    return passed_along(values, "gy", distance)


def upper_gy(values, distance):
    return passed_along(values, "gy", -distance)


def on_device(fields, inv_dx, inv_dy):
    nfield, planes, cells_x, cells_y = fields.shape
    courant = float(cells_x * lax.axis_size("gx") // 16)
    x_padded = with_halo(fields, (("gx", 2),), 2)
    y_padded = with_halo(fields, (("gy", 3),), 2)
    x_rhs = (
        x_padded[:, :, 2:-2]
        + alpha_coef * (x_padded[:, :, 1:-3] + x_padded[:, :, 3:-1])
        + beta_coef * (x_padded[:, :, :-4] + x_padded[:, :, 4:])
    )
    inverse, from_left, from_right, levels, closing, weights = line_tables(
        cells_x, lax.axis_size("gx"), courant
    )
    particular = jnp.einsum("ij,fzjy->fziy", inverse, x_rhs, precision=highest)
    edge_values = jnp.concatenate([particular[:, :, 0:2], particular[:, :, -2:]], axis=2)
    edge_values = edge_values.transpose(2, 0, 1, 3).reshape(4, -1)
    prev_tail, next_head = reduce_chain(edge_values, levels, closing, lower_gx, upper_gx)
    prev_tail = prev_tail.reshape(2, nfield, planes, cells_y)
    next_head = next_head.reshape(2, nfield, planes, cells_y)
    x_line = (
        particular
        - jnp.einsum("mi,ifzy->fzmy", from_left, prev_tail, precision=highest)
        - jnp.einsum("mi,ifzy->fzmy", from_right, next_head, precision=highest)
    )
    x_derivs = (fields - x_line) * inv_dx[None, None, :, None]
    y_rhs = (
        y_padded[:, :, :, 2:-2]
        + alpha_coef * (y_padded[:, :, :, 1:-3] + y_padded[:, :, :, 3:-1])
        + beta_coef * (y_padded[:, :, :, :-4] + y_padded[:, :, :, 4:])
    )
    inverse_y, left_y, right_y, levels_y, closing_y, weights_y = line_tables(
        cells_y, lax.axis_size("gy"), courant
    )
    particular_y = jnp.einsum("ij,fzxj->fzxi", inverse_y, y_rhs, precision=highest)
    edge_y = jnp.concatenate([particular_y[:, :, :, 0:2], particular_y[:, :, :, -2:]], axis=3)
    edge_y = edge_y.transpose(3, 0, 1, 2).reshape(4, -1)
    prev_y, next_y = reduce_chain(edge_y, levels_y, closing_y, lower_gy, upper_gy)
    prev_y = prev_y.reshape(2, nfield, planes, cells_x)
    next_y = next_y.reshape(2, nfield, planes, cells_x)
    y_line = (
        particular_y
        - jnp.einsum("mi,ifzx->fzxm", left_y, prev_y, precision=highest)
        - jnp.einsum("mi,ifzx->fzxm", right_y, next_y, precision=highest)
    )
    y_derivs = (fields - y_line) * inv_dy[None, None, None, :]
    return (x_derivs, y_derivs)


def solution(mesh):
    in_specs = (P(None, None, "gx", "gy"), P("gx"), P("gy"))
    out_specs = (P(None, None, "gx", "gy"), P(None, None, "gx", "gy"))
    return jax.shard_map(
        on_device, mesh=mesh, in_specs=in_specs, out_specs=out_specs, check_vma=False
    )
```

profile of v0, /device:TPU:1, one launch (start us, length us, event | category | flops | bytes accessed | tf_op | source)
XLA Modules:
  0.0 123.1 jit_solution(5615579520187767524)
XLA Ops:
  0.6 1.9 %fusion.50 = (f32[4,4,128,2]{3,2,1,0:T(8,128)S(1)}, f32[4,4,128,2]{3,2,1,0:T(8,128)S(1)}) fusion(f32[4,4,128,128]{3,2,1,0:T(8,128)} %param.29), kind=kLoop, calls=%fused_computation.73 | loop fusion | bytes 65536 | tf_op jit(solution)/shard_map/slice | solution.py:23
  2.6 0.3 copy.62
  2.9 4.0 %collective-permute-start.13 = (f32[4,4,128,2]{2,1,3,0:T(4,128)S(1)}, f32[4,4,128,2]{2,1,3,0:T(4,128)S(1)}, u32[]{:S(2)}, u32[]{:S(2)}) collective-permute-start(f32[4,4,128,2]{2,1,3,0:T(4,128)S(1)} %copy.62), channel_id=1, source_target_pairs={{0,1},{1,2},{2,3},{3,4},{4,5},{5,6},{6,7},{7,8},{8,9},{9,10},{10,1... | collective-permute-start | bytes 49160 | tf_op jit(solution)/shard_map/ppermute | solution.py:26
  6.9 0.3 copy.63
  7.3 5.6 %collective-permute-start.14 = (f32[4,4,128,2]{2,1,3,0:T(4,128)S(1)}, f32[4,4,128,2]{2,1,3,0:T(4,128)S(1)}, u32[]{:S(2)}, u32[]{:S(2)}) collective-permute-start(f32[4,4,128,2]{2,1,3,0:T(4,128)S(1)} %copy.63), channel_id=1, source_target_pairs={{1,0},{2,1},{3,2},{4,3},{5,4},{6,5},{7,6},{8,7},{9,8},{10,9},{11,1... | collective-permute-start | bytes 49160 | tf_op jit(solution)/shard_map/ppermute | solution.py:28
  12.9 6.5 %collective-permute-start.1 = (f32[4,4,2,128]{3,2,1,0:T(2,128)S(1)}, f32[4,4,2,128]{3,2,1,0:T(2,128)S(1)}, u32[]{:S(2)}, u32[]{:S(2)}) collective-permute-start(f32[4,4,2,128]{3,2,1,0:T(2,128)S(1)} %get-tuple-element.12), channel_id=1, source_target_pairs={{16,0},{32,16},{48,32},{64,48},{80,64},{96,80},{112,96},{128,112},... | collective-permute-start | bytes 49160 | tf_op jit(solution)/shard_map/ppermute | solution.py:28
  19.3 1.1 constant_dynamic-update-slice_fusion.1
  20.4 0.3 copy.53
  20.8 0.4 copy.46
  21.1 1.3 %copy.48 = f32[4,4,128,2]{3,2,1,0:T(8,128)} copy(f32[4,4,128,2]{2,1,3,0:T(4,128)S(1)} %collective-permute-done.14) | data formatting | bytes 32768 | tf_op jit(solution)/shard_map/ppermute | solution.py:28
  22.5 4.5 %fusion.26 = f32[4,4,128,128]{2,3,1,0:T(8,128)S(1)} fusion(f32[128,128,1,1]{1,0,3,2:T(8,128)S(1)} %copy-done.20, f32[4,4,128,128]{3,2,1,0:T(8,128)S(1)} %copy-done, f32[4,4,128,2]{3,2,1,0:T(8,128)} %copy.48, f32[4,4,128,2]{3,2,1,0:T(8,128)S(1)} %copy.46), kind=kOutput, calls=%fused_computation.45 | convolution fusion | flops 405274624 | bytes 2195456 | tf_op jit(solution)/shard_map/ij,fzxj->fzxi/dot_general | solution.py:177
  27.1 1.9 %collective-permute-start.16 = (f32[4,2048]{1,0:T(4,128)S(1)}, f32[4,2048]{1,0:T(4,128)S(1)}, u32[]{:S(2)}, u32[]{:S(2)}) collective-permute-start(f32[4,2048]{1,0:T(4,128)S(1)} %bitcast.83), channel_id=1, source_target_pairs={{0,15},{1,0},{2,1},{3,2},{4,3},{5,4},{6,5},{7,6},{8,7},{9,8},{10,9... | collective-permute-start | bytes 98312 | tf_op jit(solution)/shard_map/ppermute | solution.py:16
  29.0 3.4 %collective-permute-start.15 = (f32[4,2048]{1,0:T(4,128)S(1)}, f32[4,2048]{1,0:T(4,128)S(1)}, u32[]{:S(2)}, u32[]{:S(2)}) collective-permute-start(f32[4,2048]{1,0:T(4,128)S(1)} %bitcast.84), channel_id=1, source_target_pairs={{0,1},{1,2},{2,3},{3,4},{4,5},{5,6},{6,7},{7,8},{8,9},{9,10},{10,1... | collective-permute-start | bytes 98312 | tf_op jit(solution)/shard_map/ppermute | solution.py:16
  32.5 1.6 %convolution_bitcast_fusion = f32[4,4,128,128]{3,2,1,0:T(8,128)S(1)} fusion(f32[128,128,1,1]{1,0,3,2:T(8,128)S(1)} %copy-done.20, f32[4,4,128,128]{3,2,1,0:T(8,128)S(1)} %copy-done, f32[4,4,2,128]{3,2,1,0:T(2,128)S(1)} %collective-permute-done, f32[4,4,130,128]{3,2,1,0:T(8,128)S(1)} %constant_dynamic-update-slice_fusion), kind=kOutput, calls=%fused_computation.24 | convolution fusion | flops 404750336 | bytes 4276224 | tf_op jit(solution)/shard_map/ij,fzjy->fziy/dot_general | solution.py:157
  34.2 3.7 %collective-permute-start.3 = (f32[4,2048]{1,0:T(4,128)S(1)}, f32[4,2048]{1,0:T(4,128)S(1)}, u32[]{:S(2)}, u32[]{:S(2)}) collective-permute-start(f32[4,2048]{1,0:T(4,128)S(1)} %bitcast.86), channel_id=1, source_target_pairs={{0,496},{16,0},{32,16},{48,32},{64,48},{80,64},{96,80},{112,96},{1... | collective-permute-start | bytes 98312 | tf_op jit(solution)/shard_map/ppermute | solution.py:16
  37.9 0.2 fusion.61
  38.1 0.2 fusion.3
  38.3 3.5 %collective-permute-start.18 = (f32[4,2048]{1,0:T(4,128)S(1)}, f32[4,2048]{1,0:T(4,128)S(1)}, u32[]{:S(2)}, u32[]{:S(2)}) collective-permute-start(f32[4,2048]{1,0:T(4,128)S(1)} %fusion.3), channel_id=1, source_target_pairs={{0,14},{1,15},{2,0},{3,1},{4,2},{5,3},{6,4},{7,5},{8,6},{9,7},{10,... | collective-permute-start | bytes 98312 | tf_op jit(solution)/shard_map/ppermute | solution.py:16
  41.9 3.3 %collective-permute-start.17 = (f32[4,2048]{1,0:T(4,128)S(1)}, f32[4,2048]{1,0:T(4,128)S(1)}, u32[]{:S(2)}, u32[]{:S(2)}) collective-permute-start(f32[4,2048]{1,0:T(4,128)S(1)} %fusion.3), channel_id=1, source_target_pairs={{0,2},{1,3},{2,4},{3,5},{4,6},{5,7},{6,8},{7,9},{8,10},{9,11},{10,... | collective-permute-start | bytes 98312 | tf_op jit(solution)/shard_map/ppermute | solution.py:16
  45.1 0.2 fusion.55
  45.4 0.2 fusion.8
  45.6 7.9 %collective-permute-start.5 = (f32[4,2048]{1,0:T(4,128)S(1)}, f32[4,2048]{1,0:T(4,128)S(1)}, u32[]{:S(2)}, u32[]{:S(2)}) collective-permute-start(f32[4,2048]{1,0:T(4,128)S(1)} %fusion.8), channel_id=1, source_target_pairs={{0,480},{16,496},{32,0},{48,16},{64,32},{80,48},{96,64},{112,80},{... | collective-permute-start | bytes 98312 | tf_op jit(solution)/shard_map/ppermute | solution.py:16
  53.5 1.9 %collective-permute-start.4 = (f32[4,2048]{1,0:T(4,128)S(1)}, f32[4,2048]{1,0:T(4,128)S(1)}, u32[]{:S(2)}, u32[]{:S(2)}) collective-permute-start(f32[4,2048]{1,0:T(4,128)S(1)} %fusion.8), channel_id=1, source_target_pairs={{0,32},{16,48},{32,64},{48,80},{64,96},{80,112},{96,128},{112,144}... | collective-permute-start | bytes 98312 | tf_op jit(solution)/shard_map/ppermute | solution.py:16
  55.6 0.2 fusion.2
  55.8 2.0 %collective-permute-start.20 = (f32[4,2048]{1,0:T(4,128)S(1)}, f32[4,2048]{1,0:T(4,128)S(1)}, u32[]{:S(2)}, u32[]{:S(2)}) collective-permute-start(f32[4,2048]{1,0:T(4,128)S(1)} %fusion.2), channel_id=1, source_target_pairs={{0,12},{1,13},{2,14},{3,15},{4,0},{5,1},{6,2},{7,3},{8,4},{9,5},{1... | collective-permute-start | bytes 98312 | tf_op jit(solution)/shard_map/ppermute | solution.py:16
  57.8 3.3 %collective-permute-start.19 = (f32[4,2048]{1,0:T(4,128)S(1)}, f32[4,2048]{1,0:T(4,128)S(1)}, u32[]{:S(2)}, u32[]{:S(2)}) collective-permute-start(f32[4,2048]{1,0:T(4,128)S(1)} %fusion.2), channel_id=1, source_target_pairs={{0,4},{1,5},{2,6},{3,7},{4,8},{5,9},{6,10},{7,11},{8,12},{9,13},{1... | collective-permute-start | bytes 98312 | tf_op jit(solution)/shard_map/ppermute | solution.py:16
  61.3 0.2 fusion.7
  61.5 3.4 %collective-permute-start.7 = (f32[4,2048]{1,0:T(4,128)S(1)}, f32[4,2048]{1,0:T(4,128)S(1)}, u32[]{:S(2)}, u32[]{:S(2)}) collective-permute-start(f32[4,2048]{1,0:T(4,128)S(1)} %fusion.7), channel_id=1, source_target_pairs={{0,448},{16,464},{32,480},{48,496},{64,0},{80,16},{96,32},{112,48}... | collective-permute-start | bytes 98312 | tf_op jit(solution)/shard_map/ppermute | solution.py:16
  65.0 2.7 %collective-permute-start.6 = (f32[4,2048]{1,0:T(4,128)S(1)}, f32[4,2048]{1,0:T(4,128)S(1)}, u32[]{:S(2)}, u32[]{:S(2)}) collective-permute-start(f32[4,2048]{1,0:T(4,128)S(1)} %fusion.7), channel_id=1, source_target_pairs={{0,64},{16,80},{32,96},{48,112},{64,128},{80,144},{96,160},{112,17... | collective-permute-start | bytes 98312 | tf_op jit(solution)/shard_map/ppermute | solution.py:16
  68.0 0.2 fusion.1
  68.2 2.2 %collective-permute-start.21 = (f32[4,2048]{1,0:T(4,128)S(1)}, f32[4,2048]{1,0:T(4,128)S(1)}, u32[]{:S(2)}, u32[]{:S(2)}) collective-permute-start(f32[4,2048]{1,0:T(4,128)S(1)} %fusion.1), channel_id=1, source_target_pairs={{0,8},{1,9},{2,10},{3,11},{4,12},{5,13},{6,14},{7,15},{8,0},{9,1},... | collective-permute-start | bytes 98312 | tf_op jit(solution)/shard_map/ppermute | solution.py:16
  70.6 1.1 collective-permute-done.6
  71.9 5.5 %collective-permute-start.9 = (f32[4,2048]{1,0:T(4,128)S(1)}, f32[4,2048]{1,0:T(4,128)S(1)}, u32[]{:S(2)}, u32[]{:S(2)}) collective-permute-start(f32[4,2048]{1,0:T(4,128)S(1)} %fusion.6), channel_id=1, source_target_pairs={{0,384},{16,400},{32,416},{48,432},{64,448},{80,464},{96,480},{112... | collective-permute-start | bytes 98312 | tf_op jit(solution)/shard_map/ppermute | solution.py:16
  77.5 3.7 %collective-permute-start.8 = (f32[4,2048]{1,0:T(4,128)S(1)}, f32[4,2048]{1,0:T(4,128)S(1)}, u32[]{:S(2)}, u32[]{:S(2)}) collective-permute-start(f32[4,2048]{1,0:T(4,128)S(1)} %fusion.6), channel_id=1, source_target_pairs={{0,128},{16,144},{32,160},{48,176},{64,192},{80,208},{96,224},{112... | collective-permute-start | bytes 98312 | tf_op jit(solution)/shard_map/ppermute | solution.py:16
  81.4 0.2 fusion
  81.8 3.9 %collective-permute-start.22 = (f32[2,2048]{1,0:T(2,128)S(1)}, f32[2,2048]{1,0:T(2,128)S(1)}, u32[]{:S(2)}, u32[]{:S(2)}) collective-permute-start(f32[2,2048]{1,0:T(2,128)S(1)} %get-tuple-element.15), channel_id=1, source_target_pairs={{0,1},{1,2},{2,3},{3,4},{4,5},{5,6},{6,7},{7,8},{8,9},{9,10},{10,1... | collective-permute-start | bytes 49160 | tf_op jit(solution)/shard_map/ppermute | solution.py:16
  85.7 7.2 %collective-permute-start.23 = (f32[2,2048]{1,0:T(2,128)S(1)}, f32[2,2048]{1,0:T(2,128)S(1)}, u32[]{:S(2)}, u32[]{:S(2)}) collective-permute-start(f32[2,2048]{1,0:T(2,128)S(1)} %get-tuple-element.14), channel_id=1, source_target_pairs={{0,15},{1,0},{2,1},{3,2},{4,3},{5,4},{6,5},{7,6},{8,7},{9,8},{10,9... | collective-permute-start | bytes 49160 | tf_op jit(solution)/shard_map/ppermute | solution.py:16
  93.1 0.2 fusion.5
  93.3 8.8 %collective-permute-start.10 = (f32[4,2048]{1,0:T(4,128)S(1)}, f32[4,2048]{1,0:T(4,128)S(1)}, u32[]{:S(2)}, u32[]{:S(2)}) collective-permute-start(f32[4,2048]{1,0:T(4,128)S(1)} %fusion.5), channel_id=1, source_target_pairs={{0,256},{16,272},{32,288},{48,304},{64,320},{80,336},{96,352},{112... | collective-permute-start | bytes 98312 | tf_op jit(solution)/shard_map/ppermute | solution.py:16
  102.2 1.1 convolution_subtract_fusion.1
  103.4 3.4 %collective-permute-done.10 = f32[4,2048]{1,0:T(4,128)S(1)} collective-permute-done((f32[4,2048]{1,0:T(4,128)S(1)}, f32[4,2048]{1,0:T(4,128)S(1)}, u32[]{:S(2)}, u32[]{:S(2)}) %collective-permute-start.10) | collective-permute-done | bytes 32800 | tf_op jit(solution)/shard_map/ppermute | solution.py:16
  106.9 0.2 fusion.4
  107.4 8.1 %collective-permute-start.11 = (f32[2,2048]{1,0:T(2,128)S(1)}, f32[2,2048]{1,0:T(2,128)S(1)}, u32[]{:S(2)}, u32[]{:S(2)}) collective-permute-start(f32[2,2048]{1,0:T(2,128)S(1)} %get-tuple-element.17), channel_id=1, source_target_pairs={{0,16},{16,32},{32,48},{48,64},{64,80},{80,96},{96,112},{112,128},... | collective-permute-start | bytes 49160 | tf_op jit(solution)/shard_map/ppermute | solution.py:16
  115.5 1.1 fusion.10
  116.6 1.3 %copy.54 = f32[4,4,128,128]{3,2,1,0:T(8,128)} copy(f32[4,4,128,128]{2,3,1,0:T(8,128)S(1)} %fusion.10) | data formatting | bytes 2097152
  117.9 1.0 fusion.14
  118.9 2.1 %collective-permute-done.12 = f32[2,2048]{1,0:T(2,128)S(1)} collective-permute-done((f32[2,2048]{1,0:T(2,128)S(1)}, f32[2,2048]{1,0:T(2,128)S(1)}, u32[]{:S(2)}, u32[]{:S(2)}) %collective-permute-start.12) | collective-permute-done | bytes 16416 | tf_op jit(solution)/shard_map/ppermute | solution.py:16
  121.1 2.0 %fusion.13 = f32[4,4,128,128]{3,2,1,0:T(8,128)} fusion(f32[4,4,128,128]{3,2,1,0:T(8,128)S(1)} %copy-done, f32[4,4,128,128]{3,2,1,0:T(8,128)S(1)} %fusion.14, f32[2,4,4,128]{3,0,2,1:T(2,128)S(1)} %bitcast.92, f32[128,2,1,1]{0,1,3,2:T(2,128)S(1)} %copy-done.12, f32[128]{0:T(128)S(1)} %copy-done.19), kind=kOutput, calls=%fused_computation.30 | convolution fusion | flops 7077888 | bytes 3163648 | tf_op jit(solution)/shard_map/mi,ifzy->fzmy/dot_general | solution.py:166
  (84 shorter events, 2.2 us)
Async XLA Ops:
  2.6 10.3 %copy-start = (f32[4,4,128,128]{3,2,1,0:T(8,128)S(1)}, f32[4,4,128,128]{3,2,1,0:T(8,128)}, u32[]{:S(2)}) copy-start(f32[4,4,128,128]{3,2,1,0:T(8,128)} %param.29) | copy-start | bytes 3145732
  2.9 17.9 %collective-permute-start.13 = (f32[4,4,128,2]{2,1,3,0:T(4,128)S(1)}, f32[4,4,128,2]{2,1,3,0:T(4,128)S(1)}, u32[]{:S(2)}, u32[]{:S(2)}) collective-permute-start(f32[4,4,128,2]{2,1,3,0:T(4,128)S(1)} %copy.62), channel_id=1, source_target_pairs={{0,1},{1,2},{2,3},{3,4},{4,5},{5,6},{6,7},{7,8},{8,9},{9,10},{10,1... | collective-permute-start | bytes 49160 | tf_op jit(solution)/shard_map/ppermute | solution.py:26
  7.3 13.9 %collective-permute-start.14 = (f32[4,4,128,2]{2,1,3,0:T(4,128)S(1)}, f32[4,4,128,2]{2,1,3,0:T(4,128)S(1)}, u32[]{:S(2)}, u32[]{:S(2)}) collective-permute-start(f32[4,4,128,2]{2,1,3,0:T(4,128)S(1)} %copy.63), channel_id=1, source_target_pairs={{1,0},{2,1},{3,2},{4,3},{5,4},{6,5},{7,6},{8,7},{9,8},{10,9},{11,1... | collective-permute-start | bytes 49160 | tf_op jit(solution)/shard_map/ppermute | solution.py:28
  12.9 19.5 %collective-permute-start.1 = (f32[4,4,2,128]{3,2,1,0:T(2,128)S(1)}, f32[4,4,2,128]{3,2,1,0:T(2,128)S(1)}, u32[]{:S(2)}, u32[]{:S(2)}) collective-permute-start(f32[4,4,2,128]{3,2,1,0:T(2,128)S(1)} %get-tuple-element.12), channel_id=1, source_target_pairs={{16,0},{32,16},{48,32},{64,48},{80,64},{96,80},{112,96},{128,112},... | collective-permute-start | bytes 49160 | tf_op jit(solution)/shard_map/ppermute | solution.py:28
  19.3 13.1 %collective-permute-start = (f32[4,4,2,128]{3,2,1,0:T(2,128)S(1)}, f32[4,4,2,128]{3,2,1,0:T(2,128)S(1)}, u32[]{:S(2)}, u32[]{:S(2)}) collective-permute-start(f32[4,4,2,128]{3,2,1,0:T(2,128)S(1)} %get-tuple-element.13), channel_id=1, source_target_pairs={{0,16},{16,32},{32,48},{48,64},{64,80},{80,96},{96,112},{112,128},... | collective-permute-start | bytes 49160 | tf_op jit(solution)/shard_map/ppermute | solution.py:26
  20.7 1.8 %copy-start.20 = (f32[128,128,1,1]{1,0,3,2:T(8,128)S(1)}, f32[128,128,1,1]{1,0,3,2:T(8,128)}, u32[]{:S(2)}) copy-start(f32[128,128,1,1]{1,0,3,2:T(8,128)} %constant.49) | copy-start | bytes 196612
  22.5 9.9 %copy-start.3 = (f32[4,4,130,128]{3,2,1,0:T(8,128)S(1)}, f32[4,4,130,128]{3,2,1,0:T(8,128)}, u32[]{:S(2)}) copy-start(f32[4,4,130,128]{3,2,1,0:T(8,128)} %constant_dynamic-update-slice_fusion.1) | copy-start | bytes 3194884
  27.1 10.9 %collective-permute-start.16 = (f32[4,2048]{1,0:T(4,128)S(1)}, f32[4,2048]{1,0:T(4,128)S(1)}, u32[]{:S(2)}, u32[]{:S(2)}) collective-permute-start(f32[4,2048]{1,0:T(4,128)S(1)} %bitcast.83), channel_id=1, source_target_pairs={{0,15},{1,0},{2,1},{3,2},{4,3},{5,4},{6,5},{7,6},{8,7},{9,8},{10,9... | collective-permute-start | bytes 98312 | tf_op jit(solution)/shard_map/ppermute | solution.py:16
  29.0 9.1 %collective-permute-start.15 = (f32[4,2048]{1,0:T(4,128)S(1)}, f32[4,2048]{1,0:T(4,128)S(1)}, u32[]{:S(2)}, u32[]{:S(2)}) collective-permute-start(f32[4,2048]{1,0:T(4,128)S(1)} %bitcast.84), channel_id=1, source_target_pairs={{0,1},{1,2},{2,3},{3,4},{4,5},{5,6},{6,7},{7,8},{8,9},{9,10},{10,1... | collective-permute-start | bytes 98312 | tf_op jit(solution)/shard_map/ppermute | solution.py:16
  32.4 5.5 %copy-start.11 = (f32[4,4]{1,0:T(4,128)S(1)}, f32[4,4]{1,0:T(4,128)}, u32[]{:S(2)}) copy-start(f32[4,4]{1,0:T(4,128)} %constant.35.clone) | copy-start | bytes 196
  32.4 5.7 %copy-start.7 = (f32[4,4]{1,0:T(4,128)S(1)}, f32[4,4]{1,0:T(4,128)}, u32[]{:S(2)}) copy-start(f32[4,4]{1,0:T(4,128)} %constant.34.clone) | copy-start | bytes 196
  32.4 23.0 %copy-start.10 = (f32[4,4]{1,0:T(4,128)S(1)}, f32[4,4]{1,0:T(4,128)}, u32[]{:S(2)}) copy-start(f32[4,4]{1,0:T(4,128)} %constant.37.clone) | copy-start | bytes 196
  32.4 23.2 %copy-start.6 = (f32[4,4]{1,0:T(4,128)S(1)}, f32[4,4]{1,0:T(4,128)}, u32[]{:S(2)}) copy-start(f32[4,4]{1,0:T(4,128)} %constant.36.clone) | copy-start | bytes 196
  32.4 35.3 %copy-start.9 = (f32[4,4]{1,0:T(4,128)S(1)}, f32[4,4]{1,0:T(4,128)}, u32[]{:S(2)}) copy-start(f32[4,4]{1,0:T(4,128)} %constant.39.clone) | copy-start | bytes 196
  32.5 35.5 %copy-start.5 = (f32[4,4]{1,0:T(4,128)S(1)}, f32[4,4]{1,0:T(4,128)}, u32[]{:S(2)}) copy-start(f32[4,4]{1,0:T(4,128)} %constant.38.clone) | copy-start | bytes 196
  34.1 69.3 %copy-start.1 = (f32[4,4,128,128]{3,2,1,0:T(8,128)}, f32[4,4,128,128]{3,2,1,0:T(8,128)S(1)}, u32[]{:S(2)}) copy-start(f32[4,4,128,128]{3,2,1,0:T(8,128)S(1)} %convolution_bitcast_fusion) | copy-start | bytes 3145732
  34.1 47.1 %copy-start.8 = (f32[4,4]{1,0:T(4,128)S(1)}, f32[4,4]{1,0:T(4,128)}, u32[]{:S(2)}) copy-start(f32[4,4]{1,0:T(4,128)} %constant.41.clone) | copy-start | bytes 196
  34.1 47.3 %copy-start.4 = (f32[4,4]{1,0:T(4,128)S(1)}, f32[4,4]{1,0:T(4,128)}, u32[]{:S(2)}) copy-start(f32[4,4]{1,0:T(4,128)} %constant.40.clone) | copy-start | bytes 196
  34.1 47.5 %copy-start.17 = (f32[4,4]{1,0:T(4,128)S(1)}, f32[4,4]{1,0:T(4,128)}, u32[]{:S(2)}) copy-start(f32[4,4]{1,0:T(4,128)} %constant.48.clone) | copy-start | bytes 196
  34.1 68.1 %copy-start.13 = (f32[128,2,1,1]{0,1,3,2:T(2,128)S(1)}, f32[128,2,1,1]{0,1,3,2:T(2,128)}, u32[]{:S(2)}) copy-start(f32[128,2,1,1]{0,1,3,2:T(2,128)} %constant.50) | copy-start | bytes 3076
  34.2 11.0 %collective-permute-start.3 = (f32[4,2048]{1,0:T(4,128)S(1)}, f32[4,2048]{1,0:T(4,128)S(1)}, u32[]{:S(2)}, u32[]{:S(2)}) collective-permute-start(f32[4,2048]{1,0:T(4,128)S(1)} %bitcast.86), channel_id=1, source_target_pairs={{0,496},{16,0},{32,16},{48,32},{64,48},{80,64},{96,80},{112,96},{1... | collective-permute-start | bytes 98312 | tf_op jit(solution)/shard_map/ppermute | solution.py:16
  37.9 7.4 %collective-permute-start.2 = (f32[4,2048]{1,0:T(4,128)S(1)}, f32[4,2048]{1,0:T(4,128)S(1)}, u32[]{:S(2)}, u32[]{:S(2)}) collective-permute-start(f32[4,2048]{1,0:T(4,128)S(1)} %bitcast.87), channel_id=1, source_target_pairs={{0,16},{16,32},{32,48},{48,64},{64,80},{80,96},{96,112},{112,128},... | collective-permute-start | bytes 98312 | tf_op jit(solution)/shard_map/ppermute | solution.py:16
  38.3 17.1 %collective-permute-start.18 = (f32[4,2048]{1,0:T(4,128)S(1)}, f32[4,2048]{1,0:T(4,128)S(1)}, u32[]{:S(2)}, u32[]{:S(2)}) collective-permute-start(f32[4,2048]{1,0:T(4,128)S(1)} %fusion.3), channel_id=1, source_target_pairs={{0,14},{1,15},{2,0},{3,1},{4,2},{5,3},{6,4},{7,5},{8,6},{9,7},{10,... | collective-permute-start | bytes 98312 | tf_op jit(solution)/shard_map/ppermute | solution.py:16
  41.9 13.7 %collective-permute-start.17 = (f32[4,2048]{1,0:T(4,128)S(1)}, f32[4,2048]{1,0:T(4,128)S(1)}, u32[]{:S(2)}, u32[]{:S(2)}) collective-permute-start(f32[4,2048]{1,0:T(4,128)S(1)} %fusion.3), channel_id=1, source_target_pairs={{0,2},{1,3},{2,4},{3,5},{4,6},{5,7},{6,8},{7,9},{8,10},{9,11},{10,... | collective-permute-start | bytes 98312 | tf_op jit(solution)/shard_map/ppermute | solution.py:16
  45.6 15.6 %collective-permute-start.5 = (f32[4,2048]{1,0:T(4,128)S(1)}, f32[4,2048]{1,0:T(4,128)S(1)}, u32[]{:S(2)}, u32[]{:S(2)}) collective-permute-start(f32[4,2048]{1,0:T(4,128)S(1)} %fusion.8), channel_id=1, source_target_pairs={{0,480},{16,496},{32,0},{48,16},{64,32},{80,48},{96,64},{112,80},{... | collective-permute-start | bytes 98312 | tf_op jit(solution)/shard_map/ppermute | solution.py:16
  53.5 7.9 %collective-permute-start.4 = (f32[4,2048]{1,0:T(4,128)S(1)}, f32[4,2048]{1,0:T(4,128)S(1)}, u32[]{:S(2)}, u32[]{:S(2)}) collective-permute-start(f32[4,2048]{1,0:T(4,128)S(1)} %fusion.8), channel_id=1, source_target_pairs={{0,32},{16,48},{32,64},{48,80},{64,96},{80,112},{96,128},{112,144}... | collective-permute-start | bytes 98312 | tf_op jit(solution)/shard_map/ppermute | solution.py:16
  55.8 11.9 %collective-permute-start.20 = (f32[4,2048]{1,0:T(4,128)S(1)}, f32[4,2048]{1,0:T(4,128)S(1)}, u32[]{:S(2)}, u32[]{:S(2)}) collective-permute-start(f32[4,2048]{1,0:T(4,128)S(1)} %fusion.2), channel_id=1, source_target_pairs={{0,12},{1,13},{2,14},{3,15},{4,0},{5,1},{6,2},{7,3},{8,4},{9,5},{1... | collective-permute-start | bytes 98312 | tf_op jit(solution)/shard_map/ppermute | solution.py:16
  57.8 10.1 %collective-permute-start.19 = (f32[4,2048]{1,0:T(4,128)S(1)}, f32[4,2048]{1,0:T(4,128)S(1)}, u32[]{:S(2)}, u32[]{:S(2)}) collective-permute-start(f32[4,2048]{1,0:T(4,128)S(1)} %fusion.2), channel_id=1, source_target_pairs={{0,4},{1,5},{2,6},{3,7},{4,8},{5,9},{6,10},{7,11},{8,12},{9,13},{1... | collective-permute-start | bytes 98312 | tf_op jit(solution)/shard_map/ppermute | solution.py:16
  61.5 8.9 %collective-permute-start.7 = (f32[4,2048]{1,0:T(4,128)S(1)}, f32[4,2048]{1,0:T(4,128)S(1)}, u32[]{:S(2)}, u32[]{:S(2)}) collective-permute-start(f32[4,2048]{1,0:T(4,128)S(1)} %fusion.7), channel_id=1, source_target_pairs={{0,448},{16,464},{32,480},{48,496},{64,0},{80,16},{96,32},{112,48}... | collective-permute-start | bytes 98312 | tf_op jit(solution)/shard_map/ppermute | solution.py:16
  65.0 6.8 %collective-permute-start.6 = (f32[4,2048]{1,0:T(4,128)S(1)}, f32[4,2048]{1,0:T(4,128)S(1)}, u32[]{:S(2)}, u32[]{:S(2)}) collective-permute-start(f32[4,2048]{1,0:T(4,128)S(1)} %fusion.7), channel_id=1, source_target_pairs={{0,64},{16,80},{32,96},{48,112},{64,128},{80,144},{96,160},{112,17... | collective-permute-start | bytes 98312 | tf_op jit(solution)/shard_map/ppermute | solution.py:16
  68.2 13.0 %collective-permute-start.21 = (f32[4,2048]{1,0:T(4,128)S(1)}, f32[4,2048]{1,0:T(4,128)S(1)}, u32[]{:S(2)}, u32[]{:S(2)}) collective-permute-start(f32[4,2048]{1,0:T(4,128)S(1)} %fusion.1), channel_id=1, source_target_pairs={{0,8},{1,9},{2,10},{3,11},{4,12},{5,13},{6,14},{7,15},{8,0},{9,1},... | collective-permute-start | bytes 98312 | tf_op jit(solution)/shard_map/ppermute | solution.py:16
  71.9 21.0 %collective-permute-start.9 = (f32[4,2048]{1,0:T(4,128)S(1)}, f32[4,2048]{1,0:T(4,128)S(1)}, u32[]{:S(2)}, u32[]{:S(2)}) collective-permute-start(f32[4,2048]{1,0:T(4,128)S(1)} %fusion.6), channel_id=1, source_target_pairs={{0,384},{16,400},{32,416},{48,432},{64,448},{80,464},{96,480},{112... | collective-permute-start | bytes 98312 | tf_op jit(solution)/shard_map/ppermute | solution.py:16
  77.5 15.7 %collective-permute-start.8 = (f32[4,2048]{1,0:T(4,128)S(1)}, f32[4,2048]{1,0:T(4,128)S(1)}, u32[]{:S(2)}, u32[]{:S(2)}) collective-permute-start(f32[4,2048]{1,0:T(4,128)S(1)} %fusion.6), channel_id=1, source_target_pairs={{0,128},{16,144},{32,160},{48,176},{64,192},{80,208},{96,224},{112... | collective-permute-start | bytes 98312 | tf_op jit(solution)/shard_map/ppermute | solution.py:16
  81.8 20.4 %collective-permute-start.22 = (f32[2,2048]{1,0:T(2,128)S(1)}, f32[2,2048]{1,0:T(2,128)S(1)}, u32[]{:S(2)}, u32[]{:S(2)}) collective-permute-start(f32[2,2048]{1,0:T(2,128)S(1)} %get-tuple-element.15), channel_id=1, source_target_pairs={{0,1},{1,2},{2,3},{3,4},{4,5},{5,6},{6,7},{7,8},{8,9},{9,10},{10,1... | collective-permute-start | bytes 49160 | tf_op jit(solution)/shard_map/ppermute | solution.py:16
  85.7 29.8 %collective-permute-start.23 = (f32[2,2048]{1,0:T(2,128)S(1)}, f32[2,2048]{1,0:T(2,128)S(1)}, u32[]{:S(2)}, u32[]{:S(2)}) collective-permute-start(f32[2,2048]{1,0:T(2,128)S(1)} %get-tuple-element.14), channel_id=1, source_target_pairs={{0,15},{1,0},{2,1},{3,2},{4,3},{5,4},{6,5},{7,6},{8,7},{9,8},{10,9... | collective-permute-start | bytes 49160 | tf_op jit(solution)/shard_map/ppermute | solution.py:16
  93.1 13.6 %copy-start.16 = (f32[4,4]{1,0:T(4,128)S(1)}, f32[4,4]{1,0:T(4,128)}, u32[]{:S(2)}) copy-start(f32[4,4]{1,0:T(4,128)} %constant.43.clone) | copy-start | bytes 196
  93.3 13.6 %copy-start.14 = (f32[4,4]{1,0:T(4,128)S(1)}, f32[4,4]{1,0:T(4,128)}, u32[]{:S(2)}) copy-start(f32[4,4]{1,0:T(4,128)} %constant.42.clone) | copy-start | bytes 196
  93.3 13.4 %collective-permute-start.10 = (f32[4,2048]{1,0:T(4,128)S(1)}, f32[4,2048]{1,0:T(4,128)S(1)}, u32[]{:S(2)}, u32[]{:S(2)}) collective-permute-start(f32[4,2048]{1,0:T(4,128)S(1)} %fusion.5), channel_id=1, source_target_pairs={{0,256},{16,272},{32,288},{48,304},{64,320},{80,336},{96,352},{112... | collective-permute-start | bytes 98312 | tf_op jit(solution)/shard_map/ppermute | solution.py:16
  102.2 4.9 %copy-start.15 = (f32[4,4]{1,0:T(4,128)S(1)}, f32[4,4]{1,0:T(4,128)}, u32[]{:S(2)}) copy-start(f32[4,4]{1,0:T(4,128)} %constant.47.clone) | copy-start | bytes 196
  102.2 13.3 %copy-start.12 = (f32[128,2,1,1]{0,1,3,2:T(2,128)S(1)}, f32[128,2,1,1]{0,1,3,2:T(2,128)}, u32[]{:S(2)}) copy-start(f32[128,2,1,1]{0,1,3,2:T(2,128)} %constant.51) | copy-start | bytes 3076
  102.2 13.3 %copy-start.18 = (f32[128]{0:T(128)S(1)}, f32[128]{0:T(128)}, u32[]{:S(2)}) copy-start(f32[128]{0:T(128)} %param.31) | copy-start | bytes 1540
  107.4 10.5 %collective-permute-start.11 = (f32[2,2048]{1,0:T(2,128)S(1)}, f32[2,2048]{1,0:T(2,128)S(1)}, u32[]{:S(2)}, u32[]{:S(2)}) collective-permute-start(f32[2,2048]{1,0:T(2,128)S(1)} %get-tuple-element.17), channel_id=1, source_target_pairs={{0,16},{16,32},{32,48},{48,64},{64,80},{80,96},{96,112},{112,128},... | collective-permute-start | bytes 49160 | tf_op jit(solution)/shard_map/ppermute | solution.py:16
  116.6 1.3 %copy-start.2 = (f32[4,4,128,128]{3,2,1,0:T(8,128)S(1)}, f32[4,4,128,128]{3,2,1,0:T(8,128)}, u32[]{:S(2)}) copy-start(f32[4,4,128,128]{3,2,1,0:T(8,128)} %copy-done.1) | copy-start | bytes 3145732
  117.9 3.2 %copy-start.19 = (f32[128]{0:T(128)S(1)}, f32[128]{0:T(128)}, u32[]{:S(2)}) copy-start(f32[128]{0:T(128)} %param.30) | copy-start | bytes 1540
  117.9 3.2 %collective-permute-start.12 = (f32[2,2048]{1,0:T(2,128)S(1)}, f32[2,2048]{1,0:T(2,128)S(1)}, u32[]{:S(2)}, u32[]{:S(2)}) collective-permute-start(f32[2,2048]{1,0:T(2,128)S(1)} %get-tuple-element.16), channel_id=1, source_target_pairs={{0,496},{16,0},{32,16},{48,32},{64,48},{80,64},{96,80},{112,96},{1... | collective-permute-start | bytes 49160 | tf_op jit(solution)/shard_map/ppermute | solution.py:16
where the time goes:
time: 124 us; the launch traced here: 123 us
  starting transfers between devices  92.6 us (75%)
  matrix products  15.1 us (12%)
  local copies, waits for them, and re-layouts  7.22 us (6%)
  waiting for transfers between devices  6.65 us (5%)
  between operations  1.48 us (1%)
    ppermute x20, starting transfers between devices, passed_along(): lax.ppermute(array, axis, [(i, (i + by) % devices) for i in range(devices)])  76.6 us
    ppermute x2, starting transfers between devices, with_halo(): lax.ppermute(head, axis, [((i + 1) % count, i) for i in range(count)])  12 us
    ppermute x20, waiting for transfers between devices, passed_along(): lax.ppermute(array, axis, [(i, (i + by) % devices) for i in range(devices)])  6.64 us
    dot_general x1, matrix products, on_device(): jnp.einsum('ij,fzxj->fzxi', inverse_y, y_rhs, precision=highest)  4.5 us
    ppermute x2, starting transfers between devices, with_halo(): lax.ppermute(tail, axis, [(i, (i + 1) % count) for i in range(count)])  4.04 us
    dot_general x20, matrix products, apply_small(): return jnp.einsum('ab,bl->al', matrix, values, precision=highest)  3.81 us
    unnamed x47, local copies, waits for them, and re-layouts  3.49 us
  transfers between devices with their start and end apart: 24, of which 3 were waited for; matrix products, arithmetic and copies ran while one was open for 15% of the time, Pallas kernels for 0%

commit v1 on v0

v1 whole, which is shorter than its diff:
```python
import functools

import jax
import jax.numpy as jnp
import numpy as np
from jax import lax
from jax.experimental import pallas as pl
from jax.experimental.pallas import tpu as pltpu
from jax.sharding import PartitionSpec as P

MESH = pl.DeviceIdType.MESH
HIGHEST = lax.Precision.HIGHEST
F32 = jnp.float32
BETA = 1.0 / 36.0


def line_modes(courant):
    a, b = 4.0 / 9.0, BETA
    near, far = courant * 20.0 / 27.0, courant * 25.0 / 216.0
    top = np.array([b, a, 1.0, a, b])
    bottom = np.array([b + far, a + near, 1.0, a - near, b - far])
    roots = np.real(np.roots(bottom))
    for _ in range(4):
        roots = roots - np.polyval(bottom, roots) / np.polyval(np.polyder(bottom), roots)
    residues = np.polyval(top, roots) / np.polyval(np.polyder(bottom), roots)
    inside = sorted((k for k in range(4) if abs(roots[k]) < 1), key=lambda k: -abs(roots[k]))
    outside = sorted((k for k in range(4) if abs(roots[k]) > 1), key=lambda k: abs(roots[k]))
    forward = [(roots[k], residues[k]) for k in inside]
    backward = [(1.0 / roots[k], residues[k]) for k in outside]
    return top[0] / bottom[0], forward, backward


def tables(n, courant):
    constant, forward, backward = line_modes(courant)
    lag = np.arange(n)[:, None] - np.arange(n)[None, :]
    local = np.zeros((n, n))
    for w, r in forward:
        local += np.where(lag >= 1, r * np.power(w, np.maximum(lag - 1, 0)), 0.0)
    for v, r in backward:
        local -= np.where(lag <= 0, r * np.power(v, np.maximum(1 - lag, 0)), 0.0)
    local += constant * np.eye(n)
    i = np.arange(n)
    (w1, r1), (w3, r3) = forward
    (v2, r2), (v4, r4) = backward
    source = np.stack([r1 * w1 ** (n - 1 - i), -r2 * v2 ** (i + 2), r3 * w3 ** (n - 1 - i), -r4 * v4 ** (i + 2)])
    response = np.stack([w1**i, v2 ** (n - 1 - i), w3**i, v4 ** (n - 1 - i)])
    return local, source, response, w1**n, v2**n


def tiny_off(array):
    out = np.asarray(array, np.float32)
    return np.where(np.abs(out) < np.finfo(np.float32).tiny, np.float32(0), out)


def wait_bytes(ref, sem):
    pltpu.make_async_copy(ref, ref, sem).wait()


def exchange_kernel(q1, q2, nz, ny, planes, n,
                    fields, inv_x, inv_y, consts,
                    x_out, y_out,
                    f, cst, ixv, iyv, pre_y, coef, sx, px, pbuf, rb, gbuf, gpar, fast, sy, yb, yn,
                    load_sem, pair_s, pair_r, fast_s, fast_r, far_s, far_r, ret_s, ret_r,
                    ys_s, ys_r, yn_s, yn_r):
    gx, gy = lax.axis_index("gx"), lax.axis_index("gy")
    c, z = lax.rem(gx, 2), lax.div(gx, 2)
    half = planes // 2
    chunks = 4
    step = planes // chunks
    loads = []
    for k in range(chunks):
        loads.append(pltpu.make_async_copy(fields.at[pl.ds(k * step, step)], f.at[pl.ds(k * step, step)], load_sem.at[k]))
    loads.append(pltpu.make_async_copy(consts, cst, load_sem.at[chunks]))
    loads.append(pltpu.make_async_copy(inv_x, ixv, load_sem.at[chunks + 1]))
    loads.append(pltpu.make_async_copy(inv_y, iyv, load_sem.at[chunks + 2]))
    loads[chunks].start()
    for k in range(chunks):
        loads[k].start()
    loads[chunks + 1].start()
    loads[chunks + 2].start()

    def chip(m):
        return (lax.rem(gx + 2 * m, 2 * nz), gy)

    def along_y(m):
        return (gx, lax.rem(gy + m, ny))

    partner = (gx + 1 - 2 * c, gy)
    beside = (lax.rem(gx + 2 * nz - 1 + 2 * c, 2 * nz), gy)

    barrier = pltpu.get_barrier_semaphore()
    greeted = [chip(m) for m in range(1, nz)] + [partner, beside] + [along_y(m) for m in range(1, ny)]
    for d in greeted:
        pl.semaphore_signal(barrier, inc=1, device_id=d, device_id_type=MESH)

    loads[chunks].wait()
    row32 = lax.broadcasted_iota(jnp.int32, (32, n), 0)
    wsrc = cst[pl.ds(n, 32)]
    for h in range(2):
        acc = jnp.zeros((32, n), F32)
        for p in range(half):
            fz = h * half + p
            if fz % step == 0:
                loads[fz // step].wait()
            w = jnp.where(lax.rem(row32, half) == p, wsrc, 0.0)
            acc = acc + jnp.dot(w, f[fz], preferred_element_type=F32, precision=HIGHEST)
        for k in range(4):
            sx[k, h] = acc[k * half:(k + 1) * half]

    pl.semaphore_wait(barrier, len(greeted))

    pair = pltpu.make_async_remote_copy(sx, px, pair_s, pair_r, device_id=partner, device_id_type=MESH)
    pair.start()
    side = pltpu.make_async_remote_copy(sx.at[3 - c], fast, fast_s, fast_r, device_id=beside, device_id_type=MESH)
    side.start()
    pair.wait_recv()
    first = c == 0
    pbuf[0] = jnp.where(first, q1, 1.0) * sx[0, c] + jnp.where(first, 1.0, q1) * px[0, c]
    pbuf[1] = jnp.where(first, 1.0, q2) * sx[1, c] + jnp.where(first, q2, 1.0) * px[1, c]
    for zd in range(nz):
        @pl.when(z != zd)
        def _():
            slot = lax.rem(zd - z + nz, nz)
            pltpu.make_async_remote_copy(
                pbuf, rb.at[slot], far_s, far_r, device_id=(2 * zd + c, gy), device_id_type=MESH).start()

    for h in range(2):
        acc = jnp.zeros((32, n), F32)
        for p in range(half):
            w = jnp.where(lax.rem(row32, half) == p, wsrc, 0.0)
            acc = acc + lax.dot_general(w, f[h * half + p], (((1,), (1,)), ((), ())),
                                        preferred_element_type=F32, precision=HIGHEST)
        for k in range(4):
            sy[k, h] = acc[k * half:(k + 1) * half]
    for m in range(1, ny):
        pltpu.make_async_remote_copy(
            sy.at[pl.ds(0, 2)], yb.at[m], ys_s, ys_r, device_id=along_y(m), device_id_type=MESH).start()
    beyond = []
    for k, m in ((0, 1), (1, ny - 1)):
        copy = pltpu.make_async_remote_copy(
            sy.at[2 + k], yn.at[k], yn_s.at[k], yn_r.at[k], device_id=along_y(m), device_id_type=MESH)
        copy.start()
        beyond.append(copy)

    loads[chunks + 1].wait()
    loads[chunks + 2].wait()
    ix = jnp.transpose(jnp.broadcast_to(ixv[...], (n, n)))
    iy = iyv[...]
    for k in range(4):
        coef[k] = cst[pl.ds(n + 96, n), pl.ds(k, 1)] * ix
    coef[4] = ix
    local = cst[pl.ds(0, n)]

    def plane(fz, carry):
        cells = f[fz]
        x_out[fz] = (cells - jnp.dot(local, cells, preferred_element_type=F32, precision=HIGHEST)) * coef[4]
        y_line = lax.dot_general(cells, local, (((1,), (1,)), ((), ())), preferred_element_type=F32, precision=HIGHEST)
        pre_y[fz] = (cells - y_line) * iy
        return carry

    lax.fori_loop(0, planes, plane, 0)

    wait_bytes(yb.at[pl.ds(1, ny - 1)], ys_r)
    close1, close2 = 1.0 / (1.0 - q1**ny), 1.0 / (1.0 - q2**ny)
    fy1 = (close1 * q1 ** (ny - 1)) * sy[0]
    fy2 = (close2 * q2 ** (ny - 1)) * sy[1]
    for m in range(1, ny):
        fy1 = fy1 + (close1 * q1 ** (m - 1)) * yb[m, 0]
        fy2 = fy2 + (close2 * q2 ** (ny - m - 1)) * yb[m, 1]
    beyond[0].wait_recv()
    beyond[1].wait_recv()
    fy = jnp.concatenate([fy1.reshape(planes, n), fy2.reshape(planes, n), yn[0].reshape(planes, n),
                          yn[1].reshape(planes, n), jnp.zeros((n - 4 * planes, n), F32)], axis=0)
    fyt = jnp.transpose(fy)
    back = cst[pl.ds(n + 32, 64)] * iy
    back = jnp.concatenate([back, jnp.zeros((n - 4 * planes, n), F32)], axis=0)
    rown = lax.broadcasted_iota(jnp.int32, (n, n), 0)

    def y_plane(fz, carry):
        rhs = jnp.where(lax.rem(rown, planes) == fz, back, 0.0)
        y_out[fz] = pre_y[fz] - jnp.dot(fyt, rhs, preferred_element_type=F32, precision=HIGHEST)
        return carry

    lax.fori_loop(0, planes, y_plane, 0)

    wait_bytes(rb.at[pl.ds(1, nz - 1)], far_r)
    e1, e2 = q1 * q1, q2 * q2
    close1, close2 = 1.0 / (1.0 - e1**nz), 1.0 / (1.0 - e2**nz)
    g1 = (close1 * e1 ** (nz - 1)) * pbuf[0]
    g2 = (close2 * e2 ** (nz - 1)) * pbuf[1]
    for m in range(1, nz):
        g1 = g1 + (close1 * e1 ** (m - 1)) * rb[m, 0]
        g2 = g2 + (close2 * e2 ** (nz - m - 1)) * rb[m, 1]
    gbuf[0] = g1
    gbuf[1] = g2
    ret = pltpu.make_async_remote_copy(gbuf, gpar, ret_s, ret_r, device_id=partner, device_id_type=MESH)
    ret.start()
    side.wait_recv()
    a1 = jnp.where(first, 1.0, q1)
    b1 = jnp.where(first, 0.0, 1.0)
    a2 = jnp.where(first, q2, 1.0)
    b2 = jnp.where(first, 1.0, 0.0)
    f3 = jnp.where(first, fast[...], px[2])
    f4 = jnp.where(first, px[3], fast[...])
    ret.wait_recv()
    own1, own2, par1, par2 = gbuf[0], gbuf[1], gpar[0], gpar[1]
    for h in range(2):
        mine = c == h
        f1 = a1 * jnp.where(mine, own1, par1) + b1 * px[0, h]
        f2 = a2 * jnp.where(mine, own2, par2) + b2 * px[1, h]
        for p in range(half):
            fz = h * half + p
            fix = coef[0] * f1[p:p + 1] + coef[1] * f2[p:p + 1]
            x_out[fz] = x_out[fz] - fix - coef[2] * f3[h, p:p + 1] - coef[3] * f4[h, p:p + 1]

    pair.wait_send()
    side.wait_send()
    ret.wait_send()
    beyond[0].wait_send()
    beyond[1].wait_send()
    wait_bytes(rb.at[pl.ds(1, nz - 1)], far_s)
    wait_bytes(yb.at[pl.ds(1, ny - 1)], ys_s)


def store_kernel(x_in, y_in, x_out, y_out, sem):
    copies = [pltpu.make_async_copy(x_in, x_out, sem.at[0]), pltpu.make_async_copy(y_in, y_out, sem.at[1])]
    for copy in copies:
        copy.start()
    for copy in copies:
        copy.wait()


def on_device(fields, inv_dx, inv_dy):
    nfield, nplane, n, ncol = fields.shape
    gxn, gyn = lax.axis_size("gx"), lax.axis_size("gy")
    planes, nz = nfield * nplane, gxn // 2
    courant = float(n * gxn // 16)
    local, source, response, q1, q2 = tables(n, courant)
    half = planes // 2
    consts = np.concatenate([
        local,
        np.repeat(source, half, axis=0),
        np.repeat(response, planes, axis=0),
        np.pad(response.T, ((0, 0), (0, n - 4))),
    ], axis=0)
    consts = jnp.asarray(tiny_off(consts))
    block = jax.ShapeDtypeStruct((planes, n, n), F32)
    hbm = pl.BlockSpec(memory_space=pltpu.HBM)
    vmem = pl.BlockSpec(memory_space=pltpu.VMEM)
    vm = lambda *shape: pltpu.VMEM(shape, F32)
    dma = pltpu.SemaphoreType.DMA
    x_pre, y_pre = pl.pallas_call(
        functools.partial(exchange_kernel, float(q1), float(q2), nz, gyn, planes, n),
        out_shape=(pltpu.VMEM((planes, n, n), F32), pltpu.VMEM((planes, n, n), F32)),
        in_specs=[hbm] * 4,
        out_specs=(vmem, vmem),
        scratch_shapes=[
            vm(planes, n, n), vm(*consts.shape), vm(1, n), vm(1, n), vm(planes, n, n), vm(5, n, n),
            vm(4, 2, half, n), vm(4, 2, half, n), vm(2, half, n), vm(nz, 2, half, n), vm(2, half, n), vm(2, half, n),
            vm(2, half, n), vm(4, 2, half, n), vm(gyn, 2, 2, half, n), vm(2, 2, half, n),
            dma((7,)), dma, dma, dma, dma, dma, dma, dma, dma, dma, dma, dma((2,)), dma((2,)),
        ],
        compiler_params=pltpu.CompilerParams(
            collective_id=0, has_side_effects=True, vmem_limit_bytes=24 * 1024 * 1024),
        name="exchange",
    )(*(pltpu.with_memory_space_constraint(a, pltpu.HBM)
        for a in (fields.reshape(planes, n, n), inv_dx.reshape(1, n), inv_dy.reshape(1, n), consts)))
    x_derivs, y_derivs = pl.pallas_call(
        store_kernel,
        out_shape=(block, block),
        in_specs=[vmem, vmem],
        out_specs=(hbm, hbm),
        scratch_shapes=[dma((2,))],
        compiler_params=pltpu.CompilerParams(vmem_limit_bytes=24 * 1024 * 1024),
        name="store",
    )(x_pre, y_pre)
    return x_derivs.reshape(fields.shape), y_derivs.reshape(fields.shape)


def solution(mesh):
    spec = P(None, None, "gx", "gy")
    return jax.shard_map(
        on_device, mesh=mesh, in_specs=(spec, P("gx"), P("gy")), out_specs=(spec, spec), check_vma=False
    )
```

time: 124 us -> 33.5 us (0.27)
  starting transfers between devices: 92.6 us -> 0 us
  Pallas kernels: 0 us -> 32.7 us
  matrix products: 15.1 us -> 0 us
  local copies, waits for them, and re-layouts: 7.22 us -> 0 us
  waiting for transfers between devices: 6.65 us -> 0 us
    ppermute x24 -> x0, starting transfers between devices: 92.6 us -> none  [the longest x20 76.6 us: passed_along(): lax.ppermute(array, axis, [(i, (i + by) % devices) for i in range(devices)])]
    pallas_call x0 -> x2, Pallas kernels: none -> 32.7 us  [the longest x1 31.4 us: on_device(): pl.pallas_call(functools.partial(exchange_kernel, float(q1), float(q2), n...]
    dot_general x26 -> x0, matrix products: 15.1 us -> none  [the longest x1 4.5 us: on_device(): jnp.einsum('ij,fzxj->fzxi', inverse_y, y_rhs, precision=highest)]
    ppermute x24 -> x0, waiting for transfers between devices: 6.65 us -> none  [the longest x20 6.64 us: passed_along(): lax.ppermute(array, axis, [(i, (i + by) % devices) for i in range(devices)])]
    unnamed x47 -> x0, local copies, waits for them, and re-layouts: 3.49 us -> none
    slice x6 -> x0, local copies, waits for them, and re-layouts: 2 us -> none  [the longest x1 1.93 us: with_halo(): lax.slice_in_dim(cells, cells.shape[dim] - width, cells.shape[dim], axis=...]
    ppermute x2 -> x0, local copies, waits for them, and re-layouts: 1.71 us -> none  [the longest x1 1.35 us: with_halo(): lax.ppermute(head, axis, [((i + 1) % count, i) for i in range(count)])]
  transfers between devices with their start and end apart: 24 -> 0, of which waited for: 3 -> 0; matrix products, arithmetic and copies ran while one was open for 15% -> 0% of each run, Pallas kernels for 0% -> 0%
where the time goes in v1:
time: 33.5 us; the launch traced here: 33.4 us
  Pallas kernels  32.7 us (98%)
  between operations  0.64 us (2%)
    pallas_call x1, Pallas kernels, on_device(): pl.pallas_call(functools.partial(exchange_kernel, float(q1), float(q2), n...  31.4 us
    pallas_call x1, Pallas kernels, on_device(): pl.pallas_call(store_kernel, out_shape=(block, block), in_specs=[vmem, vm...  1.33 us

profile of v1, /device:TPU:1, one launch (start us, length us, event | category | flops | bytes accessed | tf_op | source)
XLA Modules:
  0.0 33.4 jit_solution(5050221198087700390)
XLA Ops:
  0.6 31.4 %exchange.1 = (f32[16,128,128]{2,1,0:T(8,128)S(1)}, f32[16,128,128]{2,1,0:T(8,128)S(1)}) custom-call(f32[16,128,128]{2,1,0:T(8,128)} %bitcast.5, f32[1,128]{1,0:T(1,128)} %bitcast.6, f32[1,128]{1,0:T(1,128)} %bitcast.7, f32[352,128]{1,0:T(8,128)} %constant.2.clone.consts), custom_call_target="tpu_custom_call" | custom-call | tf_op jit(solution)/shard_map/exchange/pallas_call | solution.py:252
  32.1 1.3 %store.1 = (f32[16,128,128]{2,1,0:T(8,128)}, f32[16,128,128]{2,1,0:T(8,128)}) custom-call(f32[16,128,128]{2,1,0:T(8,128)S(1)} %get-tuple-element.6.x_in, f32[16,128,128]{2,1,0:T(8,128)S(1)} %get-tuple-element.7.y_in), custom_call_target="tpu_custom_call" | custom-call | tf_op jit(solution)/shard_map/store/pallas_call | solution.py:268

commit v2 on v1

v2 whole, which is shorter than its diff:
```python
import functools

import jax
import jax.numpy as jnp
import numpy as np
from jax import lax
from jax.experimental import pallas as pl
from jax.experimental.pallas import tpu as pltpu
from jax.sharding import PartitionSpec as P

MESH = pl.DeviceIdType.MESH
HIGHEST = lax.Precision.HIGHEST
F32 = jnp.float32
BETA = 1.0 / 36.0


def line_modes(courant):
    a, b = 4.0 / 9.0, BETA
    near, far = courant * 20.0 / 27.0, courant * 25.0 / 216.0
    top = np.array([b, a, 1.0, a, b])
    bottom = np.array([b + far, a + near, 1.0, a - near, b - far])
    roots = np.real(np.roots(bottom))
    for _ in range(4):
        roots = roots - np.polyval(bottom, roots) / np.polyval(np.polyder(bottom), roots)
    residues = np.polyval(top, roots) / np.polyval(np.polyder(bottom), roots)
    inside = sorted((k for k in range(4) if abs(roots[k]) < 1), key=lambda k: -abs(roots[k]))
    outside = sorted((k for k in range(4) if abs(roots[k]) > 1), key=lambda k: abs(roots[k]))
    forward = [(roots[k], residues[k]) for k in inside]
    backward = [(1.0 / roots[k], residues[k]) for k in outside]
    return top[0] / bottom[0], forward, backward


def tables(n, courant):
    constant, forward, backward = line_modes(courant)
    lag = np.arange(n)[:, None] - np.arange(n)[None, :]
    local = np.zeros((n, n))
    for w, r in forward:
        local += np.where(lag >= 1, r * np.power(w, np.maximum(lag - 1, 0)), 0.0)
    for v, r in backward:
        local -= np.where(lag <= 0, r * np.power(v, np.maximum(1 - lag, 0)), 0.0)
    local += constant * np.eye(n)
    i = np.arange(n)
    (w1, r1), (w3, r3) = forward
    (v2, r2), (v4, r4) = backward
    source = np.stack([r1 * w1 ** (n - 1 - i), -r2 * v2 ** (i + 2), r3 * w3 ** (n - 1 - i), -r4 * v4 ** (i + 2)])
    response = np.stack([w1**i, v2 ** (n - 1 - i), w3**i, v4 ** (n - 1 - i)])
    return local, source, response, w1**n, v2**n


def tiny_off(array):
    out = np.asarray(array, np.float32)
    return np.where(np.abs(out) < np.finfo(np.float32).tiny, np.float32(0), out)


def wait_bytes(ref, sem):
    pltpu.make_async_copy(ref, ref, sem).wait()


def exchange_kernel(q1, q2, nz, ny, planes, n,
                    fields, inv_x, inv_y, consts,
                    x_out, y_out,
                    f, cst, ixv, iyv, pre_y, coef, back, sx, px, pbuf, rb, gbuf, gpar, fast, sy, yb, yn,
                    load_sem, pair_s, pair_r, fast_s, fast_r, far_s, far_r, ret_s, ret_r,
                    ys_s, ys_r, yn_s, yn_r, ready, relay):
    gx, gy = lax.axis_index("gx"), lax.axis_index("gy")
    c, z = lax.rem(gx, 2), lax.div(gx, 2)
    half, low = planes // 2, nz // 2
    early, late = z < low, z >= low
    chunks = 4
    step = planes // chunks
    loads = [pltpu.make_async_copy(consts, cst, load_sem.at[chunks])]
    for k in range(chunks):
        loads.append(pltpu.make_async_copy(fields.at[pl.ds(k * step, step)], f.at[pl.ds(k * step, step)], load_sem.at[k]))
    loads.append(pltpu.make_async_copy(inv_x, ixv, load_sem.at[chunks + 1]))
    loads.append(pltpu.make_async_copy(inv_y, iyv, load_sem.at[chunks + 2]))
    for load in loads:
        load.start()

    def chip(m):
        return (lax.rem(gx + 2 * m, 2 * nz), gy)

    def along_y(m):
        return (gx, lax.rem(gy + m, ny))

    def signal(sem, device):
        pl.semaphore_signal(sem, inc=1, device_id=device, device_id_type=MESH)

    partner = (gx + 1 - 2 * c, gy)
    beside = (lax.rem(gx + 2 * nz - 1 + 2 * c, 2 * nz), gy)

    barrier = pltpu.get_barrier_semaphore()
    signal(barrier, partner)
    signal(barrier, beside)

    @pl.when(early)
    def _():
        for m in range(1, nz):
            signal(barrier, chip(m))

    for m in range(1, ny):
        signal(barrier, along_y(m))

    def x_sources():
        rows = n + 32 + 64 + n
        w1, w2 = cst.at[pl.ds(rows, n)], cst.at[pl.ds(rows + n, n)]
        w3, w4 = cst.at[pl.ds(rows + 2 * n, n // 2)], cst.at[pl.ds(rows + 2 * n + n // 2, n // 2)]

        def total(v):
            return jnp.sum(jnp.sum(v.reshape(-1, 8, n), axis=0), axis=0, keepdims=True)

        loads[0].wait()
        for fz in range(planes):
            if fz % step == 0:
                loads[1 + fz // step].wait()
            cells = f[fz]
            h, p = fz // half, fz % half
            sx[0, h, p:p + 1] = total(cells * w1[...])
            sx[1, h, p:p + 1] = total(cells * w2[...])
            sx[2, h, p:p + 1] = total(cells[n // 2:] * w3[...])
            sx[3, h, p:p + 1] = total(cells[:n // 2] * w4[...])

    def y_sources():
        row32 = lax.broadcasted_iota(jnp.int32, (32, n), 0)
        wsrc = cst[pl.ds(n, 32)]
        for h in range(2):
            acc = jnp.zeros((32, n), F32)
            for p in range(half):
                w = jnp.where(lax.rem(row32, half) == p, wsrc, 0.0)
                acc = acc + lax.dot_general(w, f[h * half + p], (((1,), (1,)), ((), ())),
                                            preferred_element_type=F32, precision=HIGHEST)
            for k in range(4):
                sy[k, h] = acc[k * half:(k + 1) * half]

    def local_products():
        loads[chunks + 1].wait()
        loads[chunks + 2].wait()
        ix = jnp.transpose(jnp.broadcast_to(ixv[...], (n, n)))
        iy = iyv[...]
        for k in range(4):
            coef[k] = cst[pl.ds(n + 96, n), pl.ds(k, 1)] * ix
        coef[4] = ix
        local = cst[pl.ds(0, n)]
        answer = cst[pl.ds(n + 32, 4 * planes)] * iy
        top = answer.astype(jnp.bfloat16).astype(F32)
        rest = answer - top
        row = lax.rem(lax.broadcasted_iota(jnp.int32, (4 * planes, n), 0), planes)

        def plane(fz, carry):
            cells = f[fz]
            x_line = jnp.dot(local, cells, preferred_element_type=F32, precision=HIGHEST)
            x_out[fz] = (cells - x_line) * coef[4]
            y_line = lax.dot_general(cells, local, (((1,), (1,)), ((), ())),
                                     preferred_element_type=F32, precision=HIGHEST)
            pre_y[fz] = (cells - y_line) * iy
            one = jnp.where(row == fz, top, 0.0).astype(jnp.bfloat16)
            two = jnp.where(row == fz, rest, 0.0).astype(jnp.bfloat16)
            back[fz] = jnp.concatenate([one, two, one, two], axis=0)
            return carry

        lax.fori_loop(0, planes, plane, 0, unroll=4)

    def far_sends(chips):
        for zd in chips:
            @pl.when(z != zd)
            def _():
                pltpu.make_async_remote_copy(
                    pbuf, rb.at[lax.rem(zd - z + nz, nz)], far_s, far_r,
                    device_id=(2 * zd + c, gy), device_id_type=MESH).start()

    def y_sends():
        for m in range(1, ny):
            pltpu.make_async_remote_copy(
                sy.at[pl.ds(0, 2)], yb.at[m], ys_s, ys_r, device_id=along_y(m), device_id_type=MESH).start()
        for copy in beyond:
            copy.start()

    beyond = [
        pltpu.make_async_remote_copy(
            sy.at[2 + k], yn.at[k], yn_s.at[k], yn_r.at[k], device_id=along_y(m), device_id_type=MESH)
        for k, m in ((0, 1), (1, ny - 1))
    ]

    x_sources()

    @pl.when(early)
    def _():
        y_sources()
        local_products()

    pl.semaphore_wait(barrier, jnp.where(early, low - 1, low) + 2 + ny - 1)

    pair = pltpu.make_async_remote_copy(sx, px, pair_s, pair_r, device_id=partner, device_id_type=MESH)
    pair.start()

    @pl.when(late)
    def _():
        for zd in range(low):
            signal(ready, (2 * zd + c, gy))

    side = pltpu.make_async_remote_copy(sx.at[3 - c], fast, fast_s, fast_r, device_id=beside, device_id_type=MESH)
    side.start()
    pair.wait_recv()
    first = c == 0
    pbuf[0] = jnp.where(first, q1, 1.0) * sx[0, c] + jnp.where(first, 1.0, q1) * px[0, c]
    pbuf[1] = jnp.where(first, 1.0, q2) * sx[1, c] + jnp.where(first, q2, 1.0) * px[1, c]
    far_sends(range(low))

    @pl.when(late)
    def _():
        y_sources()
        y_sends()
        local_products()
        pl.semaphore_wait(relay, 1)

    @pl.when(early)
    def _():
        y_sends()
        pl.semaphore_wait(ready, nz - low)
        signal(relay, (2 * (nz - 1 - z) + c, gy))

    far_sends(range(low, nz))

    wait_bytes(yb.at[pl.ds(1, ny - 1)], ys_r)
    close1, close2 = 1.0 / (1.0 - q1**ny), 1.0 / (1.0 - q2**ny)
    fy1 = (close1 * q1 ** (ny - 1)) * sy[0]
    fy2 = (close2 * q2 ** (ny - 1)) * sy[1]
    for m in range(1, ny):
        fy1 = fy1 + (close1 * q1 ** (m - 1)) * yb[m, 0]
        fy2 = fy2 + (close2 * q2 ** (ny - m - 1)) * yb[m, 1]
    beyond[0].wait_recv()
    beyond[1].wait_recv()
    fy = jnp.concatenate([v.reshape(planes, n) for v in (fy1, fy2, yn[0], yn[1])], axis=0)
    top = fy.astype(jnp.bfloat16).astype(F32)
    rest = fy - top
    lhs = jnp.concatenate([jnp.transpose(jnp.concatenate([v, v], axis=0)) for v in (top, rest)], axis=1).astype(jnp.bfloat16)
    for fz in range(planes):
        y_out[fz] = pre_y[fz] - jnp.dot(lhs, back[fz], preferred_element_type=F32)

    wait_bytes(rb.at[pl.ds(1, nz - 1)], far_r)
    e1, e2 = q1 * q1, q2 * q2
    close1, close2 = 1.0 / (1.0 - e1**nz), 1.0 / (1.0 - e2**nz)
    g1 = (close1 * e1 ** (nz - 1)) * pbuf[0]
    g2 = (close2 * e2 ** (nz - 1)) * pbuf[1]
    for m in range(1, nz):
        g1 = g1 + (close1 * e1 ** (m - 1)) * rb[m, 0]
        g2 = g2 + (close2 * e2 ** (nz - m - 1)) * rb[m, 1]
    gbuf[0] = g1
    gbuf[1] = g2
    ret = pltpu.make_async_remote_copy(gbuf, gpar, ret_s, ret_r, device_id=partner, device_id_type=MESH)
    ret.start()
    side.wait_recv()
    a1 = jnp.where(first, 1.0, q1)
    b1 = jnp.where(first, 0.0, 1.0)
    a2 = jnp.where(first, q2, 1.0)
    b2 = jnp.where(first, 1.0, 0.0)
    f3 = jnp.where(first, fast[...], px[2])
    f4 = jnp.where(first, px[3], fast[...])
    pair.wait_send()
    side.wait_send()
    beyond[0].wait_send()
    beyond[1].wait_send()
    wait_bytes(rb.at[pl.ds(1, nz - 1)], far_s)
    wait_bytes(yb.at[pl.ds(1, ny - 1)], ys_s)
    ret.wait_recv()
    own1, own2, par1, par2 = gbuf[0], gbuf[1], gpar[0], gpar[1]
    for h in range(2):
        mine = c == h
        f1 = a1 * jnp.where(mine, own1, par1) + b1 * px[0, h]
        f2 = a2 * jnp.where(mine, own2, par2) + b2 * px[1, h]
        for p in range(half):
            fz = h * half + p
            fix = coef[0] * f1[p:p + 1] + coef[1] * f2[p:p + 1]
            x_out[fz] = x_out[fz] - fix - coef[2] * f3[h, p:p + 1] - coef[3] * f4[h, p:p + 1]
    ret.wait_send()


def store_kernel(x_in, y_in, x_out, y_out, sem):
    parts = 4
    rows = x_in.shape[0] // parts
    copies = []
    for k in range(parts):
        part = pl.ds(k * rows, rows)
        copies.append(pltpu.make_async_copy(x_in.at[part], x_out.at[part], sem.at[2 * k]))
        copies.append(pltpu.make_async_copy(y_in.at[part], y_out.at[part], sem.at[2 * k + 1]))
    for copy in copies:
        copy.start()
    for copy in copies:
        copy.wait()


def on_device(fields, inv_dx, inv_dy):
    nfield, nplane, n, ncol = fields.shape
    gxn, gyn = lax.axis_size("gx"), lax.axis_size("gy")
    planes, nz = nfield * nplane, gxn // 2
    courant = float(n * gxn // 16)
    local, source, response, q1, q2 = tables(n, courant)
    half = planes // 2
    consts = np.concatenate([
        local,
        np.repeat(source, half, axis=0),
        np.repeat(response, planes, axis=0),
        np.pad(response.T, ((0, 0), (0, n - 4))),
        np.repeat(np.concatenate([source[0], source[1], source[2, n // 2:], source[3, :n // 2]])[:, None], n, axis=1),
    ], axis=0)
    consts = jnp.asarray(tiny_off(consts))
    block = jax.ShapeDtypeStruct((planes, n, n), F32)
    hbm = pl.BlockSpec(memory_space=pltpu.HBM)
    vmem = pl.BlockSpec(memory_space=pltpu.VMEM)
    vm = lambda *shape: pltpu.VMEM(shape, F32)
    dma = pltpu.SemaphoreType.DMA
    x_pre, y_pre = pl.pallas_call(
        functools.partial(exchange_kernel, float(q1), float(q2), nz, gyn, planes, n),
        out_shape=(pltpu.VMEM((planes, n, n), F32), pltpu.VMEM((planes, n, n), F32)),
        in_specs=[hbm] * 4,
        out_specs=(vmem, vmem),
        scratch_shapes=[
            vm(planes, n, n), vm(*consts.shape), vm(1, n), vm(1, n), vm(planes, n, n), vm(5, n, n),
            pltpu.VMEM((planes, 16 * planes, n), jnp.bfloat16),
            vm(4, 2, half, n), vm(4, 2, half, n), vm(2, half, n), vm(nz, 2, half, n), vm(2, half, n), vm(2, half, n),
            vm(2, half, n), vm(4, 2, half, n), vm(gyn, 2, 2, half, n), vm(2, 2, half, n),
            dma((7,)), dma, dma, dma, dma, dma, dma, dma, dma, dma, dma, dma((2,)), dma((2,)),
            pltpu.SemaphoreType.REGULAR, pltpu.SemaphoreType.REGULAR,
        ],
        compiler_params=pltpu.CompilerParams(
            collective_id=0, has_side_effects=True, vmem_limit_bytes=24 * 1024 * 1024),
        name="exchange",
    )(*(pltpu.with_memory_space_constraint(a, pltpu.HBM)
        for a in (fields.reshape(planes, n, n), inv_dx.reshape(1, n), inv_dy.reshape(1, n), consts)))
    x_derivs, y_derivs = pl.pallas_call(
        store_kernel,
        out_shape=(block, block),
        in_specs=[vmem, vmem],
        out_specs=(hbm, hbm),
        scratch_shapes=[dma((8,))],
        compiler_params=pltpu.CompilerParams(vmem_limit_bytes=24 * 1024 * 1024),
        name="store",
    )(x_pre, y_pre)
    return x_derivs.reshape(fields.shape), y_derivs.reshape(fields.shape)


def solution(mesh):
    spec = P(None, None, "gx", "gy")
    return jax.shard_map(
        on_device, mesh=mesh, in_specs=(spec, P("gx"), P("gy")), out_specs=(spec, spec), check_vma=False
    )
```

time: 33.5 us -> 27.6 us (0.82)
  the two profiles are of different devices: /device:TPU:1 before, /device:TPU:65 now
where the time goes in v2:
time: 27.6 us; the launch traced here: 27.4 us
  Pallas kernels  26.8 us (97%)
  between operations  0.64 us (2%)
    pallas_call x1, Pallas kernels, on_device(): pl.pallas_call(functools.partial(exchange_kernel, float(q1), float(q2), n...  25.4 us
    pallas_call x1, Pallas kernels, on_device(): pl.pallas_call(store_kernel, out_shape=(block, block), in_specs=[vmem, vm...  1.38 us

profile of v2, /device:TPU:65, one launch (start us, length us, event | category | flops | bytes accessed | tf_op | source)
XLA Modules:
  0.0 27.4 jit_solution(8172042615010246489)
XLA Ops:
  0.6 25.4 %exchange.1 = (f32[16,128,128]{2,1,0:T(8,128)S(1)}, f32[16,128,128]{2,1,0:T(8,128)S(1)}) custom-call(f32[16,128,128]{2,1,0:T(8,128)} %bitcast.5, f32[1,128]{1,0:T(1,128)} %bitcast.6, f32[1,128]{1,0:T(1,128)} %bitcast.7, f32[736,128]{1,0:T(8,128)} %constant.2.clone.consts), custom_call_target="tpu_custom_call" | custom-call | tf_op jit(solution)/shard_map/exchange/pallas_call | solution.py:311
  26.0 1.4 %store.1 = (f32[16,128,128]{2,1,0:T(8,128)}, f32[16,128,128]{2,1,0:T(8,128)}) custom-call(f32[16,128,128]{2,1,0:T(8,128)S(1)} %get-tuple-element.6.x_in, f32[16,128,128]{2,1,0:T(8,128)S(1)} %get-tuple-element.7.y_in), custom_call_target="tpu_custom_call" | custom-call | tf_op jit(solution)/shard_map/store/pallas_call | solution.py:329

commit v3 on v2

--- a/solution.py
+++ b/solution.py
@@ -8,6 +8,8 @@
 from jax.experimental.pallas import tpu as pltpu
 from jax.sharding import PartitionSpec as P
 
+HUBS = ((7, 5, 0), (8, 6, 0), (9, 6, 1), (10, 12, 1), (11, 12, 0))
+TRACKS = 2
 MESH = pl.DeviceIdType.MESH
 HIGHEST = lax.Precision.HIGHEST
 F32 = jnp.float32
@@ -59,20 +61,31 @@
 def exchange_kernel(q1, q2, nz, ny, planes, n,
                     fields, inv_x, inv_y, consts,
                     x_out, y_out,
-                    f, cst, ixv, iyv, pre_y, coef, back, sx, px, pbuf, rb, gbuf, gpar, fast, sy, yb, yn,
-                    load_sem, pair_s, pair_r, fast_s, fast_r, far_s, far_r, ret_s, ret_r,
-                    ys_s, ys_r, yn_s, yn_r, ready, relay):
+                    f, cst, ixv, iyv, pre_y, coef, wx, back, sx, px, pbuf, rb, gsp, gbuf, gpar, fast, sy, yb, yn,
+                    load_sem, pair_s, pair_r, fast_s, fast_r, far_s, far_r, give_s, give_r, ret_s, ret_r,
+                    ys_s, ys_r, yn_s, yn_r, ready_y, level, relay_y):
     gx, gy = lax.axis_index("gx"), lax.axis_index("gy")
     c, z = lax.rem(gx, 2), lax.div(gx, 2)
-    half, low = planes // 2, nz // 2
-    early, late = z < low, z >= low
+    half, quarter = planes // 2, nz // 4
+    ahead, behind = z < quarter, z >= quarter
+
+    def at(chips):
+        found = z == chips[0]
+        for chip_z in chips[1:]:
+            found = found | (z == chip_z)
+        return found
+
+    spoke = at([z_of for z_of, _, _ in HUBS])
+    plain = jnp.logical_not(spoke)
     chunks = 4
     step = planes // chunks
-    loads = [pltpu.make_async_copy(consts, cst, load_sem.at[chunks])]
+    loads = [pltpu.make_async_copy(consts.at[pl.ds(0, n)], cst.at[pl.ds(0, n)], load_sem.at[chunks])]
     for k in range(chunks):
         loads.append(pltpu.make_async_copy(fields.at[pl.ds(k * step, step)], f.at[pl.ds(k * step, step)], load_sem.at[k]))
     loads.append(pltpu.make_async_copy(inv_x, ixv, load_sem.at[chunks + 1]))
     loads.append(pltpu.make_async_copy(inv_y, iyv, load_sem.at[chunks + 2]))
+    rest_rows = pl.ds(n, cst.shape[0] - n)
+    loads.append(pltpu.make_async_copy(consts.at[rest_rows], cst.at[rest_rows], load_sem.at[chunks + 3]))
     for load in loads:
         load.start()
 
@@ -82,33 +95,50 @@
     def along_y(m):
         return (gx, lax.rem(gy + m, ny))
 
+    def spoke_of(k):
+        other = 0
+        for z_of, z_hub, k_of in HUBS:
+            if k_of == k:
+                other = jnp.where(z == z_hub, z_of, other)
+        return other
+
     def signal(sem, device):
         pl.semaphore_signal(sem, inc=1, device_id=device, device_id_type=MESH)
 
     partner = (gx + 1 - 2 * c, gy)
     beside = (lax.rem(gx + 2 * nz - 1 + 2 * c, 2 * nz), gy)
 
+    hub = track = 0
+    for z_of, z_hub, k in HUBS:
+        hub, track = jnp.where(z == z_of, z_hub, hub), jnp.where(z == z_of, k, track)
     barrier = pltpu.get_barrier_semaphore()
     signal(barrier, partner)
     signal(barrier, beside)
 
-    @pl.when(early)
+    @pl.when(ahead)
     def _():
         for m in range(1, nz):
             signal(barrier, chip(m))
 
-    for m in range(1, ny):
-        signal(barrier, along_y(m))
+    for k in range(TRACKS):
+        @pl.when(at([z_hub for _, z_hub, k_of in HUBS if k_of == k]))
+        def _():
+            signal(barrier, (2 * spoke_of(k) + c, gy))
+
+    @pl.when(plain)
+    def _():
+        for m in range(1, ny):
+            signal(barrier, along_y(m))
 
     def x_sources():
-        rows = n + 32 + 64 + n
-        w1, w2 = cst.at[pl.ds(rows, n)], cst.at[pl.ds(rows + n, n)]
-        w3, w4 = cst.at[pl.ds(rows + 2 * n, n // 2)], cst.at[pl.ds(rows + 2 * n + n // 2, n // 2)]
+        loads[0].wait()
+        for k in range(4):
+            wx[k] = jnp.broadcast_to(cst[pl.ds(0, n), pl.ds(4 + k, 1)], (n, n))
+        w1, w2, w3, w4 = wx.at[0], wx.at[1], wx.at[2, pl.ds(n // 2, n // 2)], wx.at[3, pl.ds(0, n // 2)]
 
         def total(v):
             return jnp.sum(jnp.sum(v.reshape(-1, 8, n), axis=0), axis=0, keepdims=True)
 
-        loads[0].wait()
         for fz in range(planes):
             if fz % step == 0:
                 loads[1 + fz // step].wait()
@@ -121,7 +151,8 @@
 
     def y_sources():
         row32 = lax.broadcasted_iota(jnp.int32, (32, n), 0)
-        wsrc = cst[pl.ds(n, 32)]
+        loads[chunks + 3].wait()
+        wsrc = cst[pl.ds(2 * n, 32)]
         for h in range(2):
             acc = jnp.zeros((32, n), F32)
             for p in range(half):
@@ -137,10 +168,10 @@
         ix = jnp.transpose(jnp.broadcast_to(ixv[...], (n, n)))
         iy = iyv[...]
         for k in range(4):
-            coef[k] = cst[pl.ds(n + 96, n), pl.ds(k, 1)] * ix
+            coef[k] = cst[pl.ds(0, n), pl.ds(k, 1)] * ix
         coef[4] = ix
-        local = cst[pl.ds(0, n)]
-        answer = cst[pl.ds(n + 32, 4 * planes)] * iy
+        local = cst[pl.ds(n, n)]
+        answer = cst[pl.ds(2 * n + 32, 4 * planes)] * iy
         top = answer.astype(jnp.bfloat16).astype(F32)
         rest = answer - top
         row = lax.rem(lax.broadcasted_iota(jnp.int32, (4 * planes, n), 0), planes)
@@ -159,13 +190,10 @@
 
         lax.fori_loop(0, planes, plane, 0, unroll=4)
 
-    def far_sends(chips):
-        for zd in chips:
-            @pl.when(z != zd)
-            def _():
-                pltpu.make_async_remote_copy(
-                    pbuf, rb.at[lax.rem(zd - z + nz, nz)], far_s, far_r,
-                    device_id=(2 * zd + c, gy), device_id_type=MESH).start()
+    def far_send(zd):
+        pltpu.make_async_remote_copy(
+            pbuf, rb.at[lax.rem(zd - z + nz, nz)], far_s, far_r,
+            device_id=(2 * zd + c, gy), device_id_type=MESH).start()
 
     def y_sends():
         for m in range(1, ny):
@@ -180,45 +208,68 @@
         for k, m in ((0, 1), (1, ny - 1))
     ]
 
+    pair = pltpu.make_async_remote_copy(sx, px, pair_s, pair_r, device_id=partner, device_id_type=MESH)
+    side = pltpu.make_async_remote_copy(sx.at[3 - c], fast, fast_s, fast_r, device_id=beside, device_id_type=MESH)
+
+    counted = jnp.where(ahead, quarter - 1, quarter) + 2
+
+    @pl.when(spoke)
+    def _():
+        pl.semaphore_wait(barrier, counted + 1)
+        signal(ready_y.at[track], (2 * hub + c, gy))
+
     x_sources()
 
-    @pl.when(early)
+    @pl.when(plain)
     def _():
         y_sources()
-        local_products()
-
-    pl.semaphore_wait(barrier, jnp.where(early, low - 1, low) + 2 + ny - 1)
-
-    pair = pltpu.make_async_remote_copy(sx, px, pair_s, pair_r, device_id=partner, device_id_type=MESH)
+
+        @pl.when(ahead)
+        def _():
+            local_products()
+
+        pl.semaphore_wait(barrier, counted + ny - 1)
+
     pair.start()
-
-    @pl.when(late)
-    def _():
-        for zd in range(low):
-            signal(ready, (2 * zd + c, gy))
-
-    side = pltpu.make_async_remote_copy(sx.at[3 - c], fast, fast_s, fast_r, device_id=beside, device_id_type=MESH)
     side.start()
+    first = c == 0
     pair.wait_recv()
-    first = c == 0
     pbuf[0] = jnp.where(first, q1, 1.0) * sx[0, c] + jnp.where(first, 1.0, q1) * px[0, c]
     pbuf[1] = jnp.where(first, 1.0, q2) * sx[1, c] + jnp.where(first, q2, 1.0) * px[1, c]
-    far_sends(range(low))
-
-    @pl.when(late)
+    for zd in range(quarter):
+        @pl.when(z != zd)
+        def _():
+            far_send(zd)
+
+    @pl.when(plain)
+    def _():
+        y_sends()
+
+    for k in range(TRACKS):
+        @pl.when(at([z_hub for _, z_hub, k_of in HUBS if k_of == k]))
+        def _():
+            pl.semaphore_wait(ready_y.at[k], 1)
+            for m in range(1, ny):
+                signal(level.at[k], along_y(m))
+
+    for k in range(TRACKS):
+        @pl.when(at([z_hub for _, z_hub, k_of in HUBS if k_of == k]))
+        def _():
+            pl.semaphore_wait(level.at[k], ny - 1)
+            signal(relay_y, (2 * spoke_of(k) + c, gy))
+
+    @pl.when(spoke)
     def _():
         y_sources()
+
+    @pl.when(behind)
+    def _():
+        local_products()
+
+    @pl.when(spoke)
+    def _():
+        pl.semaphore_wait(relay_y, 1)
         y_sends()
-        local_products()
-        pl.semaphore_wait(relay, 1)
-
-    @pl.when(early)
-    def _():
-        y_sends()
-        pl.semaphore_wait(ready, nz - low)
-        signal(relay, (2 * (nz - 1 - z) + c, gy))
-
-    far_sends(range(low, nz))
 
     wait_bytes(yb.at[pl.ds(1, ny - 1)], ys_r)
     close1, close2 = 1.0 / (1.0 - q1**ny), 1.0 / (1.0 - q2**ny)
@@ -236,18 +287,41 @@
     for fz in range(planes):
         y_out[fz] = pre_y[fz] - jnp.dot(lhs, back[fz], preferred_element_type=F32)
 
-    wait_bytes(rb.at[pl.ds(1, nz - 1)], far_r)
     e1, e2 = q1 * q1, q2 * q2
     close1, close2 = 1.0 / (1.0 - e1**nz), 1.0 / (1.0 - e2**nz)
-    g1 = (close1 * e1 ** (nz - 1)) * pbuf[0]
-    g2 = (close2 * e2 ** (nz - 1)) * pbuf[1]
-    for m in range(1, nz):
-        g1 = g1 + (close1 * e1 ** (m - 1)) * rb[m, 0]
-        g2 = g2 + (close2 * e2 ** (nz - m - 1)) * rb[m, 1]
-    gbuf[0] = g1
-    gbuf[1] = g2
+    turns = nz // quarter
+
+    def incoming(k, to):
+        g1 = g2 = None
+        for m in range(nz):
+            shift = m + k * quarter
+            v1, v2 = (pbuf[0], pbuf[1]) if m == 0 else (rb[m, 0], rb[m, 1])
+            t1 = (close1 * e1 ** ((shift - 1) % nz)) * v1
+            t2 = (close2 * e2 ** ((-shift - 1) % nz)) * v2
+            g1, g2 = (t1, t2) if m == 0 else (g1 + t1, g2 + t2)
+        to[0] = g1
+        to[1] = g2
+
     ret = pltpu.make_async_remote_copy(gbuf, gpar, ret_s, ret_r, device_id=partner, device_id_type=MESH)
-    ret.start()
+
+    def give(k):
+        return pltpu.make_async_remote_copy(gsp.at[k - 1], gbuf, give_s, give_r,
+                                            device_id=chip(k * quarter), device_id_type=MESH)
+
+    @pl.when(ahead)
+    def _():
+        wait_bytes(rb.at[pl.ds(1, nz - 1)], far_r)
+        incoming(0, gbuf)
+        ret.start()
+        for k in range(1, turns):
+            incoming(k, gsp.at[k - 1])
+            give(k).start()
+
+    @pl.when(behind)
+    def _():
+        wait_bytes(gbuf, give_r)
+        ret.start()
+
     side.wait_recv()
     a1 = jnp.where(first, 1.0, q1)
     b1 = jnp.where(first, 0.0, 1.0)
@@ -259,7 +333,15 @@
     side.wait_send()
     beyond[0].wait_send()
     beyond[1].wait_send()
-    wait_bytes(rb.at[pl.ds(1, nz - 1)], far_s)
+
+    @pl.when(ahead)
+    def _():
+        wait_bytes(rb.at[pl.ds(0, quarter - 1)], far_s)
+
+    @pl.when(behind)
+    def _():
+        wait_bytes(rb.at[pl.ds(0, quarter)], far_s)
+
     wait_bytes(yb.at[pl.ds(1, ny - 1)], ys_s)
     ret.wait_recv()
     own1, own2, par1, par2 = gbuf[0], gbuf[1], gpar[0], gpar[1]
@@ -273,6 +355,10 @@
             x_out[fz] = x_out[fz] - fix - coef[2] * f3[h, p:p + 1] - coef[3] * f4[h, p:p + 1]
     ret.wait_send()
 
+    @pl.when(ahead)
+    def _():
+        wait_bytes(gsp, give_s)
+
 
 def store_kernel(x_in, y_in, x_out, y_out, sem):
     parts = 4
@@ -296,11 +382,10 @@
     local, source, response, q1, q2 = tables(n, courant)
     half = planes // 2
     consts = np.concatenate([
+        np.pad(np.concatenate([response, source]).T, ((0, 0), (0, n - 8))),
         local,
         np.repeat(source, half, axis=0),
         np.repeat(response, planes, axis=0),
-        np.pad(response.T, ((0, 0), (0, n - 4))),
-        np.repeat(np.concatenate([source[0], source[1], source[2, n // 2:], source[3, :n // 2]])[:, None], n, axis=1),
     ], axis=0)
     consts = jnp.asarray(tiny_off(consts))
     block = jax.ShapeDtypeStruct((planes, n, n), F32)
@@ -314,12 +399,12 @@
         in_specs=[hbm] * 4,
         out_specs=(vmem, vmem),
         scratch_shapes=[
-            vm(planes, n, n), vm(*consts.shape), vm(1, n), vm(1, n), vm(planes, n, n), vm(5, n, n),
+            vm(planes, n, n), vm(*consts.shape), vm(1, n), vm(1, n), vm(planes, n, n), vm(5, n, n), vm(4, n, n),
             pltpu.VMEM((planes, 16 * planes, n), jnp.bfloat16),
-            vm(4, 2, half, n), vm(4, 2, half, n), vm(2, half, n), vm(nz, 2, half, n), vm(2, half, n), vm(2, half, n),
+            vm(4, 2, half, n), vm(4, 2, half, n), vm(2, half, n), vm(nz, 2, half, n), vm(3, 2, half, n), vm(2, half, n), vm(2, half, n),
             vm(2, half, n), vm(4, 2, half, n), vm(gyn, 2, 2, half, n), vm(2, 2, half, n),
-            dma((7,)), dma, dma, dma, dma, dma, dma, dma, dma, dma, dma, dma((2,)), dma((2,)),
-            pltpu.SemaphoreType.REGULAR, pltpu.SemaphoreType.REGULAR,
+            dma((8,)), dma, dma, dma, dma, dma, dma, dma, dma, dma, dma, dma, dma, dma((2,)), dma((2,)),
+            pltpu.SemaphoreType.REGULAR((TRACKS,)), pltpu.SemaphoreType.REGULAR((TRACKS,)), pltpu.SemaphoreType.REGULAR,
         ],
         compiler_params=pltpu.CompilerParams(
             collective_id=0, has_side_effects=True, vmem_limit_bytes=24 * 1024 * 1024),

time: 27.6 us -> 25.1 us (0.909)
  the two profiles are of different devices: /device:TPU:65 before, /device:TPU:1 now
where the time goes in v3:
time: 25.1 us; the launch traced here: 24.6 us
  Pallas kernels  24 us (96%)
  between operations  0.64 us (3%)
    pallas_call x1, Pallas kernels, on_device(): pl.pallas_call(functools.partial(exchange_kernel, float(q1), float(q2), n...  22.6 us
    pallas_call x1, Pallas kernels, on_device(): pl.pallas_call(store_kernel, out_shape=(block, block), in_specs=[vmem, vm...  1.38 us

profile of v3, /device:TPU:1, one launch (start us, length us, event | category | flops | bytes accessed | tf_op | source)
XLA Modules:
  0.0 24.6 jit_solution(11164556756267141365)
XLA Ops:
  0.6 22.6 %exchange.1 = (f32[16,128,128]{2,1,0:T(8,128)S(1)}, f32[16,128,128]{2,1,0:T(8,128)S(1)}) custom-call(f32[16,128,128]{2,1,0:T(8,128)} %bitcast.5, f32[1,128]{1,0:T(1,128)} %bitcast.6, f32[1,128]{1,0:T(1,128)} %bitcast.7, f32[352,128]{1,0:T(8,128)} %constant.2.clone.consts), custom_call_target="tpu_custom_call" | custom-call | tf_op jit(solution)/shard_map/exchange/pallas_call | solution.py:396
  23.3 1.4 %store.1 = (f32[16,128,128]{2,1,0:T(8,128)}, f32[16,128,128]{2,1,0:T(8,128)}) custom-call(f32[16,128,128]{2,1,0:T(8,128)S(1)} %get-tuple-element.6.x_in, f32[16,128,128]{2,1,0:T(8,128)S(1)} %get-tuple-element.7.y_in), custom_call_target="tpu_custom_call" | custom-call | tf_op jit(solution)/shard_map/store/pallas_call | solution.py:414

commit v4 on v3

--- a/solution.py
+++ b/solution.py
@@ -8,8 +8,8 @@
 from jax.experimental.pallas import tpu as pltpu
 from jax.sharding import PartitionSpec as P
 
-HUBS = ((7, 5, 0), (8, 6, 0), (9, 6, 1), (10, 12, 1), (11, 12, 0))
-TRACKS = 2
+HUBS = ((7, 5, 0), (8, 6, 0), (9, 6, 1), (10, 13, 2), (11, 13, 1), (12, 13, 0))
+TRACKS = 3
 MESH = pl.DeviceIdType.MESH
 HIGHEST = lax.Precision.HIGHEST
 F32 = jnp.float32
@@ -213,12 +213,12 @@
 
     counted = jnp.where(ahead, quarter - 1, quarter) + 2
 
+    x_sources()
+
     @pl.when(spoke)
     def _():
         pl.semaphore_wait(barrier, counted + 1)
         signal(ready_y.at[track], (2 * hub + c, gy))
-
-    x_sources()
 
     @pl.when(plain)
     def _():
@@ -230,8 +230,19 @@
 
         pl.semaphore_wait(barrier, counted + ny - 1)
 
+    def hear_spokes(among):
+        for k in range(TRACKS):
+            hubs = [z_hub for _, z_hub, k_of in HUBS if k_of == k and among(z_hub)]
+            if hubs:
+                @pl.when(at(hubs))
+                def _():
+                    pl.semaphore_wait(ready_y.at[k], 1)
+                    for m in range(1, ny):
+                        signal(level.at[k], along_y(m))
+
     pair.start()
     side.start()
+    hear_spokes(lambda z_hub: z_hub >= nz // 2)
     first = c == 0
     pair.wait_recv()
     pbuf[0] = jnp.where(first, q1, 1.0) * sx[0, c] + jnp.where(first, 1.0, q1) * px[0, c]
@@ -245,12 +256,7 @@
     def _():
         y_sends()
 
-    for k in range(TRACKS):
-        @pl.when(at([z_hub for _, z_hub, k_of in HUBS if k_of == k]))
-        def _():
-            pl.semaphore_wait(ready_y.at[k], 1)
-            for m in range(1, ny):
-                signal(level.at[k], along_y(m))
+    hear_spokes(lambda z_hub: z_hub < nz // 2)
 
     for k in range(TRACKS):
         @pl.when(at([z_hub for _, z_hub, k_of in HUBS if k_of == k]))
@@ -313,7 +319,7 @@
         wait_bytes(rb.at[pl.ds(1, nz - 1)], far_r)
         incoming(0, gbuf)
         ret.start()
-        for k in range(1, turns):
+        for k in sorted(range(1, turns), key=lambda k: -min(k, turns - k)):
             incoming(k, gsp.at[k - 1])
             give(k).start()
 

time: 25.1 us -> 24.8 us (0.988); the launches traced: 24.6 us -> 24.6 us
  no operation moved by 1% of the time
where the time goes in v4:
time: 24.8 us; the launch traced here: 24.6 us
  Pallas kernels  24 us (97%)
  between operations  0.64 us (3%)
    pallas_call x1, Pallas kernels, on_device(): pl.pallas_call(functools.partial(exchange_kernel, float(q1), float(q2), n...  22.6 us
    pallas_call x1, Pallas kernels, on_device(): pl.pallas_call(store_kernel, out_shape=(block, block), in_specs=[vmem, vm...  1.38 us

profile of v4, /device:TPU:1, one launch (start us, length us, event | category | flops | bytes accessed | tf_op | source)
XLA Modules:
  0.0 24.6 jit_solution(3695069126742822067)
XLA Ops:
  0.6 22.6 %exchange.1 = (f32[16,128,128]{2,1,0:T(8,128)S(1)}, f32[16,128,128]{2,1,0:T(8,128)S(1)}) custom-call(f32[16,128,128]{2,1,0:T(8,128)} %bitcast.5, f32[1,128]{1,0:T(1,128)} %bitcast.6, f32[1,128]{1,0:T(1,128)} %bitcast.7, f32[352,128]{1,0:T(8,128)} %constant.2.clone.consts), custom_call_target="tpu_custom_call" | custom-call | tf_op jit(solution)/shard_map/exchange/pallas_call | solution.py:402
  23.3 1.4 %store.1 = (f32[16,128,128]{2,1,0:T(8,128)}, f32[16,128,128]{2,1,0:T(8,128)}) custom-call(f32[16,128,128]{2,1,0:T(8,128)S(1)} %get-tuple-element.6.x_in, f32[16,128,128]{2,1,0:T(8,128)S(1)} %get-tuple-element.7.y_in), custom_call_target="tpu_custom_call" | custom-call | tf_op jit(solution)/shard_map/store/pallas_call | solution.py:420

commit v5 on v4

--- a/solution.py
+++ b/solution.py
@@ -32,36 +32,38 @@
     return top[0] / bottom[0], forward, backward
 
 
-def tables(n, courant):
-    constant, forward, backward = line_modes(courant)
-    lag = np.arange(n)[:, None] - np.arange(n)[None, :]
-    local = np.zeros((n, n))
-    for w, r in forward:
-        local += np.where(lag >= 1, r * np.power(w, np.maximum(lag - 1, 0)), 0.0)
-    for v, r in backward:
-        local -= np.where(lag <= 0, r * np.power(v, np.maximum(1 - lag, 0)), 0.0)
-    local += constant * np.eye(n)
-    i = np.arange(n)
-    (w1, r1), (w3, r3) = forward
-    (v2, r2), (v4, r4) = backward
-    source = np.stack([r1 * w1 ** (n - 1 - i), -r2 * v2 ** (i + 2), r3 * w3 ** (n - 1 - i), -r4 * v4 ** (i + 2)])
-    response = np.stack([w1**i, v2 ** (n - 1 - i), w3**i, v4 ** (n - 1 - i)])
-    return local, source, response, w1**n, v2**n
-
-
-def tiny_off(array):
-    out = np.asarray(array, np.float32)
-    return np.where(np.abs(out) < np.finfo(np.float32).tiny, np.float32(0), out)
+def power(root, exponent):
+    size = jnp.exp(exponent.astype(F32) * float(np.log(abs(root))))
+    return size if root > 0 else jnp.where(lax.rem(exponent, 2) == 1, -size, size)
+
+
+def sources(modes, n, i):
+    _, ((w1, r1), (w3, r3)), ((v2, r2), (v4, r4)) = modes
+    return (float(r1) * power(w1, n - 1 - i), float(-r2) * power(v2, i + 2),
+            float(r3) * power(w3, n - 1 - i), float(-r4) * power(v4, i + 2))
+
+
+def responses(modes, n, i):
+    _, ((w1, _), (w3, _)), ((v2, _), (v4, _)) = modes
+    return power(w1, i), power(v2, n - 1 - i), power(w3, i), power(v4, n - 1 - i)
+
+
+def local_table(modes, lag):
+    constant, ((w1, r1), (w3, r3)), ((v2, r2), (v4, r4)) = modes
+    up, down = jnp.maximum(lag - 1, 0), jnp.maximum(1 - lag, 0)
+    above = float(r1) * power(w1, up) + float(r3) * power(w3, up)
+    below = float(-r2) * power(v2, down) + float(-r4) * power(v4, down)
+    return jnp.where(lag >= 1, above, below) + jnp.where(lag == 0, float(constant), 0.0)
 
 
 def wait_bytes(ref, sem):
     pltpu.make_async_copy(ref, ref, sem).wait()
 
 
-def exchange_kernel(q1, q2, nz, ny, planes, n,
-                    fields, inv_x, inv_y, consts,
+def exchange_kernel(modes, q1, q2, nz, ny, planes, n,
+                    fields, inv_x, inv_y,
                     x_out, y_out,
-                    f, cst, ixv, iyv, pre_y, coef, wx, back, sx, px, pbuf, rb, gsp, gbuf, gpar, fast, sy, yb, yn,
+                    f, ixv, iyv, pre_y, coef, wx, back, sx, px, pbuf, rb, gsp, gbuf, gpar, fast, sy, yb, yn,
                     load_sem, pair_s, pair_r, fast_s, fast_r, far_s, far_r, give_s, give_r, ret_s, ret_r,
                     ys_s, ys_r, yn_s, yn_r, ready_y, level, relay_y):
     gx, gy = lax.axis_index("gx"), lax.axis_index("gy")
@@ -79,13 +81,11 @@
     plain = jnp.logical_not(spoke)
     chunks = 4
     step = planes // chunks
-    loads = [pltpu.make_async_copy(consts.at[pl.ds(0, n)], cst.at[pl.ds(0, n)], load_sem.at[chunks])]
+    loads = []
     for k in range(chunks):
         loads.append(pltpu.make_async_copy(fields.at[pl.ds(k * step, step)], f.at[pl.ds(k * step, step)], load_sem.at[k]))
     loads.append(pltpu.make_async_copy(inv_x, ixv, load_sem.at[chunks + 1]))
     loads.append(pltpu.make_async_copy(inv_y, iyv, load_sem.at[chunks + 2]))
-    rest_rows = pl.ds(n, cst.shape[0] - n)
-    loads.append(pltpu.make_async_copy(consts.at[rest_rows], cst.at[rest_rows], load_sem.at[chunks + 3]))
     for load in loads:
         load.start()
 
@@ -130,10 +130,11 @@
         for m in range(1, ny):
             signal(barrier, along_y(m))
 
+    row, col = (lax.broadcasted_iota(jnp.int32, (n, n), d) for d in (0, 1))
+
     def x_sources():
-        loads[0].wait()
-        for k in range(4):
-            wx[k] = jnp.broadcast_to(cst[pl.ds(0, n), pl.ds(4 + k, 1)], (n, n))
+        for k, weights in enumerate(sources(modes, n, row)):
+            wx[k] = weights
         w1, w2, w3, w4 = wx.at[0], wx.at[1], wx.at[2, pl.ds(n // 2, n // 2)], wx.at[3, pl.ds(0, n // 2)]
 
         def total(v):
@@ -141,7 +142,7 @@
 
         for fz in range(planes):
             if fz % step == 0:
-                loads[1 + fz // step].wait()
+                loads[fz // step].wait()
             cells = f[fz]
             h, p = fz // half, fz % half
             sx[0, h, p:p + 1] = total(cells * w1[...])
@@ -151,8 +152,7 @@
 
     def y_sources():
         row32 = lax.broadcasted_iota(jnp.int32, (32, n), 0)
-        loads[chunks + 3].wait()
-        wsrc = cst[pl.ds(2 * n, 32)]
+        wsrc = jnp.concatenate(sources(modes, n, col[:half]), axis=0)
         for h in range(2):
             acc = jnp.zeros((32, n), F32)
             for p in range(half):
@@ -163,18 +163,18 @@
                 sy[k, h] = acc[k * half:(k + 1) * half]
 
     def local_products():
+        loads[chunks].wait()
         loads[chunks + 1].wait()
-        loads[chunks + 2].wait()
         ix = jnp.transpose(jnp.broadcast_to(ixv[...], (n, n)))
         iy = iyv[...]
-        for k in range(4):
-            coef[k] = cst[pl.ds(0, n), pl.ds(k, 1)] * ix
+        for k, weights in enumerate(responses(modes, n, row)):
+            coef[k] = weights * ix
         coef[4] = ix
-        local = cst[pl.ds(n, n)]
-        answer = cst[pl.ds(2 * n + 32, 4 * planes)] * iy
+        local = local_table(modes, row - col)
+        answer = jnp.concatenate(responses(modes, n, col[:planes]), axis=0) * iy
         top = answer.astype(jnp.bfloat16).astype(F32)
         rest = answer - top
-        row = lax.rem(lax.broadcasted_iota(jnp.int32, (4 * planes, n), 0), planes)
+        own = lax.rem(lax.broadcasted_iota(jnp.int32, (4 * planes, n), 0), planes)
 
         def plane(fz, carry):
             cells = f[fz]
@@ -183,8 +183,8 @@
             y_line = lax.dot_general(cells, local, (((1,), (1,)), ((), ())),
                                      preferred_element_type=F32, precision=HIGHEST)
             pre_y[fz] = (cells - y_line) * iy
-            one = jnp.where(row == fz, top, 0.0).astype(jnp.bfloat16)
-            two = jnp.where(row == fz, rest, 0.0).astype(jnp.bfloat16)
+            one = jnp.where(own == fz, top, 0.0).astype(jnp.bfloat16)
+            two = jnp.where(own == fz, rest, 0.0).astype(jnp.bfloat16)
             back[fz] = jnp.concatenate([one, two, one, two], axis=0)
             return carry
 
@@ -385,27 +385,21 @@
     gxn, gyn = lax.axis_size("gx"), lax.axis_size("gy")
     planes, nz = nfield * nplane, gxn // 2
     courant = float(n * gxn // 16)
-    local, source, response, q1, q2 = tables(n, courant)
+    modes = line_modes(courant)
+    q1, q2 = (mode[0][0] ** n for mode in modes[1:])
     half = planes // 2
-    consts = np.concatenate([
-        np.pad(np.concatenate([response, source]).T, ((0, 0), (0, n - 8))),
-        local,
-        np.repeat(source, half, axis=0),
-        np.repeat(response, planes, axis=0),
-    ], axis=0)
-    consts = jnp.asarray(tiny_off(consts))
     block = jax.ShapeDtypeStruct((planes, n, n), F32)
     hbm = pl.BlockSpec(memory_space=pltpu.HBM)
     vmem = pl.BlockSpec(memory_space=pltpu.VMEM)
     vm = lambda *shape: pltpu.VMEM(shape, F32)
     dma = pltpu.SemaphoreType.DMA
     x_pre, y_pre = pl.pallas_call(
-        functools.partial(exchange_kernel, float(q1), float(q2), nz, gyn, planes, n),
+        functools.partial(exchange_kernel, modes, float(q1), float(q2), nz, gyn, planes, n),
         out_shape=(pltpu.VMEM((planes, n, n), F32), pltpu.VMEM((planes, n, n), F32)),
-        in_specs=[hbm] * 4,
+        in_specs=[hbm] * 3,
         out_specs=(vmem, vmem),
         scratch_shapes=[
-            vm(planes, n, n), vm(*consts.shape), vm(1, n), vm(1, n), vm(planes, n, n), vm(5, n, n), vm(4, n, n),
+            vm(planes, n, n), vm(1, n), vm(1, n), vm(planes, n, n), vm(5, n, n), vm(4, n, n),
             pltpu.VMEM((planes, 16 * planes, n), jnp.bfloat16),
             vm(4, 2, half, n), vm(4, 2, half, n), vm(2, half, n), vm(nz, 2, half, n), vm(3, 2, half, n), vm(2, half, n), vm(2, half, n),
             vm(2, half, n), vm(4, 2, half, n), vm(gyn, 2, 2, half, n), vm(2, 2, half, n),
@@ -416,7 +410,7 @@
             collective_id=0, has_side_effects=True, vmem_limit_bytes=24 * 1024 * 1024),
         name="exchange",
     )(*(pltpu.with_memory_space_constraint(a, pltpu.HBM)
-        for a in (fields.reshape(planes, n, n), inv_dx.reshape(1, n), inv_dy.reshape(1, n), consts)))
+        for a in (fields.reshape(planes, n, n), inv_dx.reshape(1, n), inv_dy.reshape(1, n))))
     x_derivs, y_derivs = pl.pallas_call(
         store_kernel,
         out_shape=(block, block),

time: 24.8 us -> 24.8 us (level)
  no operation moved by 1% of the time
where the time goes in v5:
time: 24.8 us; the launch traced here: 24.6 us
  Pallas kernels  24 us (97%)
  between operations  0.64 us (3%)
    pallas_call x1, Pallas kernels, on_device(): pl.pallas_call(functools.partial(exchange_kernel, modes, float(q1), float...  22.6 us
    pallas_call x1, Pallas kernels, on_device(): pl.pallas_call(store_kernel, out_shape=(block, block), in_specs=[vmem, vm...  1.38 us

profile of v5, /device:TPU:1, one launch (start us, length us, event | category | flops | bytes accessed | tf_op | source)
XLA Modules:
  0.0 24.6 jit_solution(16427637670098363593)
XLA Ops:
  0.6 22.6 %exchange.1 = (f32[16,128,128]{2,1,0:T(8,128)S(1)}, f32[16,128,128]{2,1,0:T(8,128)S(1)}) custom-call(f32[16,128,128]{2,1,0:T(8,128)} %bitcast.5, f32[1,128]{1,0:T(1,128)} %bitcast.6, f32[1,128]{1,0:T(1,128)} %bitcast.7), custom_call_target="tpu_custom_call" | custom-call | tf_op jit(solution)/shard_map/exchange/pallas_call | solution.py:396
  23.3 1.4 %store.1 = (f32[16,128,128]{2,1,0:T(8,128)}, f32[16,128,128]{2,1,0:T(8,128)}) custom-call(f32[16,128,128]{2,1,0:T(8,128)S(1)} %get-tuple-element.6.x_in, f32[16,128,128]{2,1,0:T(8,128)S(1)} %get-tuple-element.7.y_in), custom_call_target="tpu_custom_call" | custom-call | tf_op jit(solution)/shard_map/store/pallas_call | solution.py:414
